TPU v7x, 256 devices: a whole 4x4x8 slice. The times are simulated.
256 devices in a mesh: plane: 16 (over z, x_lo), elem: 16 (over x_hi, y, core).
Axes of the slice: x: 4 (x_hi: 2, x_lo: 2; x = x_hi * 2 + x_lo), y: 4, z: 8, core: 2. Of those that a mesh axis runs over, the one named last changes fastest.
Arguments:
- velocity_modes: float32 [2, 3, 1024, 16384], P(None, None, 'plane', 'elem'), may hold values from -1.5 to 1.5
- geometry: float32 [4, 16384], P(None, 'elem'), may hold values from -4 to 4
- neighbour: int32 [256, 4], P('elem'), may hold values from -1 to 255, as said below
- neighbour_edge: int32 [256, 4], P('elem'), may hold values from 0 to 3, as said below
- flipped: int32 [256, 4], P('elem'), may hold values from 0 to 1
Outputs:
- advection: float32 [2, 3, 1024, 16384], P(None, None, 'plane', 'elem')
Inputs may be any that keep to these rules, and one draw needn't show every extreme that they name: Element e belongs to index e // 16 of elem. Every neighbour belongs to the same index or to the one before or after it, cyclically. Neighbours are mutual: if edge k of a meets edge k2 of b, edge k2 of b meets edge k of a. `neighbour_edge`: 0 where neighbour is -1.
All inputs are finite; a program needn't handle non-finite values.
Results may differ from a plain program's by a relative error of at most 0.00015.
Values sent between devices are 32-bit elements; how exact they have to be, the bound alone decides.
A program may use at most 64 MiB of HBM per device.

v0:
```python
import math

import jax
import jax.numpy as jnp
import numpy as np
from jax import lax
from jax.sharding import PartitionSpec as P

PLANES = 1024
POINTS = 64


span_wave = 2.0
highest = lax.Precision.HIGHEST
gll_nodes = [
    -1.0,
    -0.8717401485096066,
    -0.5917001814331423,
    -0.2092992179024789,
    0.2092992179024789,
    0.5917001814331423,
    0.8717401485096066,
    1.0,
]


def partner_2(block, axis, bit):
    count = lax.axis_size(axis)
    route = []
    for low in range(count):
        high = low | 1 << bit
        if high != low and high < count:
            route += [(low, high), (high, low)]
    return lax.ppermute(block, axis, route)


def extended(x, sides, width):
    for axis, dim in sides:
        count, length = (lax.axis_size(axis), x.shape[dim])
        up = [(i, (i + 1) % count) for i in range(count)]
        down = [(j, i) for i, j in up]
        last = lax.slice_in_dim(x, length - width, length, axis=dim)
        initial = lax.slice_in_dim(x, 0, width, axis=dim)
        before = lax.ppermute(last, axis, up)
        after = lax.ppermute(initial, axis, down)
        x = jnp.concatenate([before, x, after], axis=dim)
    return x


def legendre_seven(point_value):
    earlier_value = 1.0
    current_value = point_value
    for degree_index in range(1, 7):
        next_value = (
            (2 * degree_index + 1) * point_value * current_value - degree_index * earlier_value
        ) / (degree_index + 1)
        earlier_value = current_value
        current_value = next_value
    return current_value


def gll_matrices():
    legendre_vals = [legendre_seven(node_value) for node_value in gll_nodes]
    deriv_matrix = np.zeros((8, 8))
    for row_index in range(8):
        for col_index in range(8):
            if row_index != col_index:
                deriv_matrix[row_index, col_index] = (
                    legendre_vals[row_index]
                    / legendre_vals[col_index]
                    / (gll_nodes[row_index] - gll_nodes[col_index])
                )
    deriv_matrix[0, 0] = -14.0
    deriv_matrix[7, 7] = 14.0
    identity = np.eye(8)
    return (np.kron(identity, deriv_matrix), np.kron(deriv_matrix, identity))


def edge_interior(field):
    return jnp.stack(
        [field[..., 0, 1:7], field[..., 1:7, 7], field[..., 7, 1:7], field[..., 1:7, 0]], axis=-2
    )


def put_edges(field, edges):
    field = field.at[..., 0, 1:7].set(edges[..., 0, :])
    field = field.at[..., 1:7, 7].set(edges[..., 1, :])
    field = field.at[..., 7, 1:7].set(edges[..., 2, :])
    return field.at[..., 1:7, 0].set(edges[..., 3, :])


def rotate(complex_pair, phase_angle):
    cosine = jnp.cos(phase_angle)
    sine_part = jnp.sin(phase_angle)
    return jnp.stack(
        [
            cosine * complex_pair[0] - sine_part * complex_pair[1],
            sine_part * complex_pair[0] + cosine * complex_pair[1],
        ]
    )


def bit_reverse(plane_index, n_bits):
    result = jnp.zeros((), jnp.int32)
    for bit_pos in range(n_bits):
        result = result + (plane_index >> bit_pos & 1) * (1 << n_bits - 1 - bit_pos)
    return result


def spread_pairs(stacked, plane_index, n_bits):
    for bit_pos in reversed(range(n_bits)):
        upper_bit = plane_index >> bit_pos & 1
        lower_bits = plane_index & (1 << bit_pos) - 1
        parity_sign = (1 - 2 * upper_bit).astype(jnp.float32)
        partner = partner_2(stacked, "plane", bit_pos)
        phase_angle = (
            2.0 * math.pi / 2 ** (bit_pos + 1) * (upper_bit * lower_bits).astype(jnp.float32)
        )
        stacked = rotate(partner + parity_sign * stacked, phase_angle)
    return stacked


def fold_pairs(stacked, plane_index, n_bits):
    for bit_pos in range(n_bits):
        upper_bit = plane_index >> bit_pos & 1
        lower_bits = plane_index & (1 << bit_pos) - 1
        parity_sign = (1 - 2 * upper_bit).astype(jnp.float32)
        phase_angle = (
            2.0 * math.pi / 2 ** (bit_pos + 1) * (upper_bit * lower_bits).astype(jnp.float32)
        )
        turned = rotate(stacked, -phase_angle)
        partner = partner_2(turned, "plane", bit_pos)
        stacked = 0.5 * (partner + parity_sign * turned)
    return stacked


def local_tables(plane_pos, planes_dev):
    local_ids = jnp.arange(planes_dev, dtype=jnp.int32)
    twist = (plane_pos * local_ids % PLANES).astype(jnp.float32) * (2.0 * math.pi / PLANES)
    grid_ids = local_ids[:, None] * local_ids[None, :] % planes_dev
    table = grid_ids.astype(jnp.float32) * (2.0 * math.pi / planes_dev)
    return (twist[:, None], jnp.cos(table), jnp.sin(table))


def local_inverse(stacked, plane_pos, planes_dev):
    twist, cosine, sine_part = local_tables(plane_pos, planes_dev)
    turned = rotate(stacked, twist)
    return jnp.einsum("bm,fmc->fbc", cosine, turned[0], precision=highest) - jnp.einsum(
        "bm,fmc->fbc", sine_part, turned[1], precision=highest
    )


def local_forward(field, plane_pos, planes_dev):
    twist, cosine, sine_part = local_tables(plane_pos, planes_dev)
    real_part = jnp.einsum("bm,fbc->fmc", cosine, field, precision=highest) / planes_dev
    imag_part = -jnp.einsum("bm,fbc->fmc", sine_part, field, precision=highest) / planes_dev
    return rotate(jnp.stack([real_part, imag_part]), -twist)


def make_spectral(velocity_modes, plane_index, planes_dev):
    global_ids = plane_index * planes_dev + jnp.arange(planes_dev, dtype=jnp.int32)
    signed = jnp.where(global_ids < PLANES // 2, global_ids, global_ids - PLANES)
    wave_factor = (span_wave * signed.astype(jnp.float32))[None, :, None]
    span_modes = jnp.stack([-wave_factor * velocity_modes[1], wave_factor * velocity_modes[0]])
    return jnp.concatenate([velocity_modes, span_modes], axis=1)


def shards(velocity_modes, geometry, neighbour, neighbour_edge, flipped):
    planes_dev = velocity_modes.shape[2]
    columns = velocity_modes.shape[3]
    elem_dev = columns // POINTS
    blocks = columns // 128
    n_bits = lax.axis_size("plane").bit_length() - 1
    plane_index = lax.axis_index("plane")
    spread = spread_pairs(
        make_spectral(velocity_modes, plane_index, planes_dev), plane_index, n_bits
    )
    plane_pos = bit_reverse(plane_index, n_bits)
    physical = local_inverse(spread, plane_pos, planes_dev)
    xi_table, eta_table = gll_matrices()
    xi_pair = jnp.asarray(np.kron(np.eye(2), xi_table), jnp.float32)
    eta_pair = jnp.asarray(np.kron(np.eye(2), eta_table), jnp.float32)
    velocity = physical[:3].reshape(3, planes_dev, blocks, 128)
    along_xi = jnp.einsum("flbq,rq->flbr", velocity, xi_pair, precision=highest)
    along_eta = jnp.einsum("flbq,rq->flbr", velocity, eta_pair, precision=highest)
    metric = geometry.reshape(4, blocks, 128)
    grad_x = metric[0] * along_xi + metric[1] * along_eta
    grad_y = metric[2] * along_xi + metric[3] * along_eta
    cells = jnp.stack([grad_x, grad_y], axis=1).reshape(6, planes_dev, elem_dev, 8, 8)
    own_edges = edge_interior(cells)
    traces = jnp.transpose(own_edges, (2, 3, 4, 0, 1)).reshape(elem_dev * 4, 6, 6 * planes_dev)
    safe_ids = jnp.maximum(neighbour, 0)
    table_rows = extended(traces, (("elem", 0),), elem_dev * 4)
    offset = (safe_ids // elem_dev - lax.axis_index("elem")) % lax.axis_size("elem")
    block_ids = jnp.where(offset == 0, 1, jnp.where(offset == 1, 2, 0))
    row_ids = (block_ids * elem_dev + safe_ids % elem_dev) * 4 + neighbour_edge
    far_edges = jnp.take(table_rows, row_ids.reshape(-1), axis=0)
    far_edges = jnp.where(flipped.reshape(-1)[:, None, None] == 1, far_edges[:, ::-1, :], far_edges)
    averaged = jnp.where(
        neighbour.reshape(-1)[:, None, None] >= 0, 0.5 * (traces + far_edges), traces
    )
    restored = jnp.transpose(averaged.reshape(elem_dev, 4, 6, 6, planes_dev), (3, 4, 0, 1, 2))
    gradients = put_edges(cells, restored).reshape(6, planes_dev, columns)
    nonlinear = (
        physical[0] * gradients[0::2] + physical[1] * gradients[1::2] + physical[2] * physical[3:]
    )
    spectrum = local_forward(nonlinear, plane_pos, planes_dev)
    advection = fold_pairs(spectrum, plane_index, n_bits)
    return advection


def solution(mesh):
    placed = (
        P(None, None, "plane", "elem"),
        P(None, "elem"),
        P("elem", None),
        P("elem", None),
        P("elem", None),
    )
    return jax.shard_map(
        shards,
        mesh=mesh,
        in_specs=placed,
        out_specs=P(None, None, "plane", "elem"),
        check_vma=False,
    )
```

profile of v0, /device:TPU:8, one launch (start us, length us, event | category | flops | bytes accessed | tf_op | source)
XLA Modules:
  0.0 751.6 jit_solution(15352729038918961524)
XLA Ops:
  0.0 1.7 slice_multiply_fusion.2
  1.9 1.8 maximum_maximum_fusion
  3.7 7.2 collective-permute-start
  11.1 135.1 %collective-permute-done = f32[2,6,64,1024]{3,2,1,0:T(8,128)} collective-permute-done((f32[2,6,64,1024]{3,2,1,0:T(8,128)}, f32[2,6,64,1024]{3,2,1,0:T(8,128)}, u32[]{:S(2)}, u32[]{:S(2)}) %collective-permute-start) | collective-permute-done | bytes 3145760 | tf_op jit(solution)/shard_map/ppermute | solution.py:34
  146.2 2.6 multiply_add_fusion.3
  148.8 0.4 multiply_subtract_fusion.3
  149.2 1.8 pad_maximum_fusion
  151.1 2.6 collective-permute-start.1
  153.9 135.0 %collective-permute-done.1 = f32[2,6,64,1024]{3,2,1,0:T(8,128)} collective-permute-done((f32[2,6,64,1024]{3,2,1,0:T(8,128)}, f32[2,6,64,1024]{3,2,1,0:T(8,128)}, u32[]{:S(2)}, u32[]{:S(2)}) %collective-permute-start.1) | collective-permute-done | bytes 3145760 | tf_op jit(solution)/shard_map/ppermute | solution.py:34
  288.9 2.6 multiply_add_fusion.2
  292.0 1.8 pad_maximum_fusion.1
  294.0 68.9 %collective-permute-done.2 = f32[2,6,64,1024]{3,2,1,0:T(8,128)} collective-permute-done((f32[2,6,64,1024]{3,2,1,0:T(8,128)}, f32[2,6,64,1024]{3,2,1,0:T(8,128)}, u32[]{:S(2)}, u32[]{:S(2)}) %collective-permute-start.2) | collective-permute-done | bytes 3145760 | tf_op jit(solution)/shard_map/ppermute | solution.py:34
  362.9 2.6 multiply_add_fusion.1
  365.9 1.8 pad_maximum_fusion.2
  367.8 1.5 collective-permute-start.3
  369.6 66.3 %collective-permute-done.3 = f32[2,6,64,1024]{3,2,1,0:T(8,128)} collective-permute-done((f32[2,6,64,1024]{3,2,1,0:T(8,128)}, f32[2,6,64,1024]{3,2,1,0:T(8,128)}, u32[]{:S(2)}, u32[]{:S(2)}) %collective-permute-start.3) | collective-permute-done | bytes 3145760 | tf_op jit(solution)/shard_map/ppermute | solution.py:34
  435.9 2.6 multiply_add_fusion
  438.5 2.1 fusion
  440.6 2.2 subtract_bitcast_fusion
  443.1 0.9 copy-done.1
  444.0 0.8 fusion.10
  444.8 0.8 add_bitcast_fusion.1
  445.7 1.3 pad_maximum_fusion.4
  447.0 2.1 copy.62
  449.9 1.9 copy.67
  451.8 2.6 reshape.320
  454.3 1.7 collective-permute-start.5
  456.6 0.6 fusion.76
  457.2 1.4 copy.74
  458.7 2.0 slice_bitcast_fusion.6
  460.7 3.3 collective-permute-done.4
  464.0 1.4 copy.70
  465.4 1.4 copy.72
  466.8 1.6 pad_maximum_fusion.3
  468.5 3.1 gather_fusion
  471.6 2.2 broadcast_select_fusion
  473.8 3.0 rev.3
  476.7 2.9 multiply_select_fusion
  479.6 2.7 reshape.343
  482.3 1.7 copy.102
  484.0 0.9 slice_bitcast_fusion.2
  484.9 1.0 copy.78
  486.0 1.0 copy.80
  487.0 6.0 scatter.14
  493.0 9.9 %scatter.15 = f32[6,64,16,8,8]{1,4,3,2,0:T(8,128)S(1)} dynamic-update-slice(f32[6,64,16,8,8]{1,4,3,2,0:T(8,128)S(1)} %scatter.14, f32[6,64,16,6,1]{1,4,3,2,0:T(1,128)} %copy.78, s32[]{:T(128)} %constant.239.clone.1, s32[]{:T(128)} %constant.239.clone.1, s32[]{:T(128)} %constant.239.clone.1, s32[]{:T(128)} %constant.233.clone.1, s32[]{:T(128)} %constant.234.clone.1) | dynamic-update-slice | bytes 294916 | tf_op jit(solution)/shard_map/scatter | solution.py:87
  502.9 4.1 scatter.16
  507.0 9.9 %scatter.19 = f32[6,64,16,8,8]{1,4,3,2,0:T(8,128)S(1)} dynamic-update-slice(f32[6,64,16,8,8]{1,4,3,2,0:T(8,128)S(1)} %scatter.16, f32[6,64,16,6,1]{1,4,3,2,0:T(1,128)} %copy.80, s32[]{:T(128)} %constant.239.clone.1, s32[]{:T(128)} %constant.239.clone.1, s32[]{:T(128)} %constant.239.clone.1, s32[]{:T(128)} %constant.233.clone.1, s32[]{:T(128)} %constant.239.clone.1) | dynamic-update-slice | bytes 294916 | tf_op jit(solution)/shard_map/scatter | solution.py:89
  516.9 1.8 fusion.72
  518.7 2.9 copy.95
  521.6 1.3 copy.96
  523.2 1.8 fusion.14
  525.0 0.9 convolution_negate_fusion
  525.9 1.2 fusion.16
  527.1 1.2 pad_maximum_fusion.5
  528.3 1.5 collective-permute-start.6
  530.0 35.1 %collective-permute-done.6 = f32[2,3,64,1024]{3,2,1,0:T(8,128)S(1)} collective-permute-done((f32[2,3,64,1024]{3,2,1,0:T(8,128)}, f32[2,3,64,1024]{3,2,1,0:T(8,128)S(1)}, u32[]{:S(2)}, u32[]{:S(2)}) %collective-permute-start.6) | collective-permute-done | bytes 1572896 | tf_op jit(solution)/shard_map/ppermute | solution.py:34
  565.7 1.2 pad_maximum_fusion.6
  567.0 0.6 collective-permute-start.7
  567.7 35.2 %collective-permute-done.7 = f32[2,3,64,1024]{3,2,1,0:T(8,128)S(1)} collective-permute-done((f32[2,3,64,1024]{3,2,1,0:T(8,128)}, f32[2,3,64,1024]{3,2,1,0:T(8,128)S(1)}, u32[]{:S(2)}, u32[]{:S(2)}) %collective-permute-start.7) | collective-permute-done | bytes 1572896 | tf_op jit(solution)/shard_map/ppermute | solution.py:34
  603.5 1.2 pad_maximum_fusion.7
  604.9 69.5 %collective-permute-done.8 = f32[2,3,64,1024]{3,2,1,0:T(8,128)S(1)} collective-permute-done((f32[2,3,64,1024]{3,2,1,0:T(8,128)}, f32[2,3,64,1024]{3,2,1,0:T(8,128)S(1)}, u32[]{:S(2)}, u32[]{:S(2)}) %collective-permute-start.8) | collective-permute-done | bytes 1572896 | tf_op jit(solution)/shard_map/ppermute | solution.py:34
  675.2 7.0 collective-permute-start.9
  682.2 67.9 %collective-permute-done.9 = f32[2,3,64,1024]{3,2,1,0:T(8,128)S(1)} collective-permute-done((f32[2,3,64,1024]{3,2,1,0:T(8,128)S(1)}, f32[2,3,64,1024]{3,2,1,0:T(8,128)S(1)}, u32[]{:S(2)}, u32[]{:S(2)}) %collective-permute-start.9) | collective-permute-done | bytes 1572896 | tf_op jit(solution)/shard_map/ppermute | solution.py:34
  750.2 1.4 add_multiply_fusion
  (59 shorter events, 5.0 us)
Async XLA Ops:
  0.0 1.9 copy-start
  3.7 142.5 %collective-permute-start = (f32[2,6,64,1024]{3,2,1,0:T(8,128)}, f32[2,6,64,1024]{3,2,1,0:T(8,128)}, u32[]{:S(2)}, u32[]{:S(2)}) collective-permute-start(f32[2,6,64,1024]{3,2,1,0:T(8,128)} %maximum_maximum_fusion), channel_id=1, source_target_pairs={{0,128},{128,0},{16,144},{144,16},{32,160},{160,32},{48,176},{176,... | collective-permute-start | bytes 9437192 | tf_op jit(solution)/shard_map/ppermute | solution.py:34
  151.1 137.8 %collective-permute-start.1 = (f32[2,6,64,1024]{3,2,1,0:T(8,128)}, f32[2,6,64,1024]{3,2,1,0:T(8,128)}, u32[]{:S(2)}, u32[]{:S(2)}) collective-permute-start(f32[2,6,64,1024]{3,2,1,0:T(8,128)} %pad_maximum_fusion), channel_id=1, source_target_pairs={{0,64},{64,0},{16,80},{80,16},{32,96},{96,32},{48,112},{112,48},{1... | collective-permute-start | bytes 9437192 | tf_op jit(solution)/shard_map/ppermute | solution.py:34
  293.8 69.1 %collective-permute-start.2 = (f32[2,6,64,1024]{3,2,1,0:T(8,128)}, f32[2,6,64,1024]{3,2,1,0:T(8,128)}, u32[]{:S(2)}, u32[]{:S(2)}) collective-permute-start(f32[2,6,64,1024]{3,2,1,0:T(8,128)} %pad_maximum_fusion.1), channel_id=1, source_target_pairs={{0,32},{32,0},{16,48},{48,16},{64,96},{96,64},{80,112},{112,80},{1... | collective-permute-start | bytes 9437192 | tf_op jit(solution)/shard_map/ppermute | solution.py:34
  365.9 3.4 copy-start.8
  365.9 3.4 copy-start.10
  365.9 3.7 copy-start.9
  365.9 3.7 copy-start.7
  367.8 68.1 %collective-permute-start.3 = (f32[2,6,64,1024]{3,2,1,0:T(8,128)}, f32[2,6,64,1024]{3,2,1,0:T(8,128)}, u32[]{:S(2)}, u32[]{:S(2)}) collective-permute-start(f32[2,6,64,1024]{3,2,1,0:T(8,128)} %pad_maximum_fusion.2), channel_id=1, source_target_pairs={{0,16},{16,0},{32,48},{48,32},{64,80},{80,64},{96,112},{112,96},{1... | collective-permute-start | bytes 9437192 | tf_op jit(solution)/shard_map/ppermute | solution.py:34
  442.9 1.1 copy-start.1
  442.9 1.1 copy-start.6
  443.0 1.9 copy-start.5
  454.3 9.6 %collective-permute-start.4 = (f32[64,6,384]{2,0,1:T(8,128)}, f32[64,6,384]{2,0,1:T(8,128)}, u32[]{:S(2)}, u32[]{:S(2)}) collective-permute-start(f32[64,6,384]{2,0,1:T(8,128)} %reshape.320), channel_id=1, source_target_pairs={{0,1},{1,2},{2,3},{3,4},{4,5},{5,6},{6,7},{7,8},{8,9},{9,10},{10,1... | collective-permute-start | bytes 1769480 | tf_op jit(solution)/shard_map/ppermute | solution.py:44
  454.3 11.0 %collective-permute-start.5 = (f32[64,6,384]{2,0,1:T(8,128)}, f32[64,6,384]{2,0,1:T(8,128)}, u32[]{:S(2)}, u32[]{:S(2)}) collective-permute-start(f32[64,6,384]{2,0,1:T(8,128)} %reshape.320), channel_id=1, source_target_pairs={{1,0},{2,1},{3,2},{4,3},{5,4},{6,5},{7,6},{8,7},{9,8},{10,9},{11,1... | collective-permute-start | bytes 1769480 | tf_op jit(solution)/shard_map/ppermute | solution.py:45
  518.7 2.9 copy-start.3
  521.6 1.4 copy-start.2
  521.6 1.6 copy-start.4
  528.3 36.8 %collective-permute-start.6 = (f32[2,3,64,1024]{3,2,1,0:T(8,128)}, f32[2,3,64,1024]{3,2,1,0:T(8,128)S(1)}, u32[]{:S(2)}, u32[]{:S(2)}) collective-permute-start(f32[2,3,64,1024]{3,2,1,0:T(8,128)} %pad_maximum_fusion.5), channel_id=1, source_target_pairs={{0,16},{16,0},{32,48},{48,32},{64,80},{80,64},{96,112},{112,96},{1... | collective-permute-start | bytes 4718600 | tf_op jit(solution)/shard_map/ppermute | solution.py:34
  567.0 36.0 %collective-permute-start.7 = (f32[2,3,64,1024]{3,2,1,0:T(8,128)}, f32[2,3,64,1024]{3,2,1,0:T(8,128)S(1)}, u32[]{:S(2)}, u32[]{:S(2)}) collective-permute-start(f32[2,3,64,1024]{3,2,1,0:T(8,128)} %pad_maximum_fusion.6), channel_id=1, source_target_pairs={{0,32},{32,0},{16,48},{48,16},{64,96},{96,64},{80,112},{112,80},{1... | collective-permute-start | bytes 4718600 | tf_op jit(solution)/shard_map/ppermute | solution.py:34
  604.8 69.6 %collective-permute-start.8 = (f32[2,3,64,1024]{3,2,1,0:T(8,128)}, f32[2,3,64,1024]{3,2,1,0:T(8,128)S(1)}, u32[]{:S(2)}, u32[]{:S(2)}) collective-permute-start(f32[2,3,64,1024]{3,2,1,0:T(8,128)} %pad_maximum_fusion.7), channel_id=1, source_target_pairs={{0,64},{64,0},{16,80},{80,16},{32,96},{96,32},{48,112},{112,48},{1... | collective-permute-start | bytes 4718600 | tf_op jit(solution)/shard_map/ppermute | solution.py:34
  675.2 75.0 %collective-permute-start.9 = (f32[2,3,64,1024]{3,2,1,0:T(8,128)S(1)}, f32[2,3,64,1024]{3,2,1,0:T(8,128)S(1)}, u32[]{:S(2)}, u32[]{:S(2)}) collective-permute-start(f32[2,3,64,1024]{3,2,1,0:T(8,128)S(1)} %pad_maximum_fusion.8), channel_id=1, source_target_pairs={{0,128},{128,0},{16,144},{144,16},{32,160},{160,32},{48,176},{176,... | collective-permute-start | bytes 4718600 | tf_op jit(solution)/shard_map/ppermute | solution.py:34
where the time goes:
time: 756 us; the launch traced here: 752 us
  waiting for transfers between devices  616 us (81%)
  local copies, waits for them, and re-layouts  65.5 us (9%)
  other arithmetic  38 us (5%)
  starting transfers between devices  22.2 us (3%)
  matrix products  8.06 us (1%)
    ppermute x8, waiting for transfers between devices, partner_2(): return lax.ppermute(block, axis, route)  613 us
    ppermute x8, starting transfers between devices, partner_2(): return lax.ppermute(block, axis, route)  20.4 us
  transfers between devices with their start and end apart: 10, of which 9 were waited for; matrix products, arithmetic and copies ran while one was open for 1% of the time, Pallas kernels for 0%

commit v1 on v0

v1 whole, which is shorter than its diff:
```python
import jax
import jax.numpy as jnp
import ml_dtypes
import numpy as np
from jax import lax
from jax.experimental import pallas as pl
from jax.experimental.pallas import tpu as pltpu
from jax.sharding import PartitionSpec as P

PLANES = 1024
POINTS = 64
MESH = pl.DeviceIdType.MESH
highest = lax.Precision.HIGHEST
gll_nodes = [
    -1.0,
    -0.8717401485096066,
    -0.5917001814331423,
    -0.2092992179024789,
    0.2092992179024789,
    0.5917001814331423,
    0.8717401485096066,
    1.0,
]


def legendre_seven(point_value):
    earlier_value = 1.0
    current_value = point_value
    for degree_index in range(1, 7):
        next_value = (
            (2 * degree_index + 1) * point_value * current_value - degree_index * earlier_value
        ) / (degree_index + 1)
        earlier_value = current_value
        current_value = next_value
    return current_value


def gll_matrices():
    legendre_vals = [legendre_seven(node_value) for node_value in gll_nodes]
    deriv_matrix = np.zeros((8, 8))
    for row_index in range(8):
        for col_index in range(8):
            if row_index != col_index:
                deriv_matrix[row_index, col_index] = (
                    legendre_vals[row_index]
                    / legendre_vals[col_index]
                    / (gll_nodes[row_index] - gll_nodes[col_index])
                )
    deriv_matrix[0, 0] = -14.0
    deriv_matrix[7, 7] = 14.0
    identity = np.eye(8)
    return (np.kron(identity, deriv_matrix), np.kron(deriv_matrix, identity))


def halves(matrix):
    high = matrix.astype(ml_dtypes.bfloat16)
    low = (matrix - high.astype(np.float64)).astype(ml_dtypes.bfloat16)
    return high, low


def point_order():
    steps = range(1, 7)
    order = [p for p in steps] + [8 * p + 7 for p in steps]
    order += [56 + p for p in steps] + [8 * p for p in steps]
    return order + [r for r in range(POINTS) if r not in order]


def tables():
    order = point_order()
    xi, eta = gll_matrices()
    eye = np.eye(POINTS)[order]
    pair = np.kron(np.eye(2), eye)
    edge_xi = np.kron(np.eye(2), xi[order[:24]])
    edge_eta = np.kron(np.eye(2), eta[order[:24]])
    pack_high, pack_low = halves(np.concatenate([pair, edge_xi, edge_eta]))
    pack_low = pack_low[128:]
    edge_pick = np.kron(np.eye(2), eye[:24]).astype(np.float32)

    k = (64 * np.arange(8)[:, None] + np.arange(64)[None, :])[:, None, :]
    waves = []
    for block in range(4):
        plane = 2 * (256 * (block % 2) + np.arange(256)) + block // 2
        angle = (k[..., None] * plane) % PLANES * (2.0 * np.pi / PLANES)
        waves.append(np.concatenate([np.cos(angle), -np.sin(angle)], axis=1).reshape(1024, 256))
    wave_high, wave_low = halves(np.stack(waves))

    mode = 64 * np.arange(16)[:, None] + np.arange(64)[None, :]
    factor = 2.0 * np.where(mode < 512, mode, mode - 1024)
    factor = np.concatenate([-factor, factor], axis=1).astype(np.float32)[:, None, :]

    own_xi = xi[order][:, order].astype(np.float32)
    own_eta = eta[order][:, order].astype(np.float32)

    row = np.arange(384)
    owner = (row[:, None] // 24 == np.arange(16)).astype(np.float32)
    edge = (row[:, None] % 24 // 6 == np.arange(4)).astype(np.float32)
    place = (row % 6).astype(np.float32)[:, None]
    edge_own = np.concatenate([edge[:24], np.zeros((40, 4), np.float32)])

    def unpack(points):
        out = np.zeros((2, 3, len(points), 3, 128))
        for side in range(2):
            for field in range(3):
                for r, point in enumerate(points):
                    out[side, field, r, field, 64 * side + point] = 1.0
        return out.reshape(6 * len(points), 384).astype(ml_dtypes.bfloat16)

    return dict(
        pack_high=pack_high,
        pack_low=pack_low,
        edge_pick=edge_pick,
        pair=pair.astype(np.float32),
        factor=factor,
        own_xi=own_xi,
        own_eta=own_eta,
        owner=owner,
        edge=edge,
        place=place,
        edge_own=edge_own,
        unpack_edge=unpack(order[:24]),
        unpack_rest=unpack(order[24:]),
        wave_high=wave_high,
        wave_low=wave_low,
    )


def split(x):
    high = x.astype(jnp.bfloat16)
    return high, (x - high.astype(jnp.float32)).astype(jnp.bfloat16)


def mm(a, b, dims=((1,), (0,))):
    return lax.dot_general(a, b, (dims, ((), ())), preferred_element_type=jnp.float32)


NT = ((1,), (1,))
TN = ((0,), (0,))


def mm3(a, b, dims=((1,), (0,))):
    return mm(a[0], b[0], dims) + (mm(a[0], b[1], dims) + mm(a[1], b[0], dims))


def exact(a, b, dims=((1,), (0,))):
    return lax.dot_general(
        a, b, (dims, ((), ())), precision=highest, preferred_element_type=jnp.float32
    )


def kernel(
    modes, geometry, neighbour, neighbour_edge, flipped,
    pack_high, pack_low, edge_pick, pair, factor, own_xi, own_eta, owner, edge, place, edge_own,
    unpack_edge, unpack_rest, wave_high_hbm, wave_low_hbm,
    out,
    wave_high, wave_low, geo_column, send_vel, recv_vel, traces, far, recv_far, left_high, left_low,
    left_edge, rest, own_edge, uv_edge, total_rest, total_edge, send_rest, recv_rest, send_edge, recv_edge,
    wave_sem, trace_send, trace_recv, vel_s, vel_r, far_s, far_r, rest_s, rest_r, edge_s, edge_r,
):
    me = lax.axis_index("plane")
    group = lax.axis_index("elem")
    z = me // 2
    x = me % 2

    def peer(i):
        h = i // 2
        dz = (h + 1) // 2 * (2 * (h % 2) - 1)
        return (z + dz + 8) % 8 * 2 + (x + i) % 2

    loads = [
        pltpu.make_async_copy(wave_high_hbm, wave_high, wave_sem.at[0]),
        pltpu.make_async_copy(wave_low_hbm, wave_low, wave_sem.at[1]),
    ]
    for load in loads:
        load.start()

    barrier = pltpu.get_barrier_semaphore()

    def greet(i, carry):
        pl.semaphore_signal(barrier, inc=1, device_id={"plane": peer(i)}, device_id_type=MESH)
        return carry

    lax.fori_loop(1, 16, greet, 0)
    before = (group + 15) % 16
    after = (group + 1) % 16
    for other in (before, after):
        pl.semaphore_signal(barrier, inc=1, device_id={"elem": other}, device_id_type=MESH)
    pl.semaphore_wait(barrier, 17)

    def pack(q):
        cols = pl.ds(pl.multiple_of(128 * q, 128), 128)
        block = jnp.concatenate(
            [modes[c, f, :, cols] for f in range(3) for c in range(2)], axis=0
        )
        high, low = split(block)
        both = mm(pack_high[...], high, NT) + mm(pack_high[...], low, NT)
        send_vel[q] = both[:128]
        along = both[128:] + mm(pack_low[...], high, NT)
        geo = exact(edge_pick[...], geometry[:, cols], NT)
        rows = pl.ds(pl.multiple_of(48 * q, 16), 48)
        traces[rows, :384] = geo[:, 0:1] * along[:48] + geo[:, 1:2] * along[48:]
        traces[rows, 384:] = geo[:, 2:3] * along[:48] + geo[:, 3:4] * along[48:]

    def vel_part(p):
        return send_vel.at[p // 2, pl.ds(pl.multiple_of(p % 2 * 64, 64), 64)]

    def vel_copy(p, slot):
        return pltpu.make_async_remote_copy(
            vel_part(p), recv_vel.at[slot], vel_s.at[p], vel_r.at[slot],
            device_id={"plane": p}, device_id_type=MESH,
        )

    pack(z)
    vel_copy(peer(1), me).start()
    recv_vel[me] = send_vel[z, pl.ds(pl.multiple_of(x * 64, 64), 64), :]

    def pack_step(h, carry):
        pack(peer(2 * h) // 2)
        vel_copy(peer(2 * h), me).start()
        vel_copy(peer(2 * h + 1), me).start()
        return carry

    lax.fori_loop(1, 8, pack_step, 0)

    def trace_copy(slot, other):
        return pltpu.make_async_remote_copy(
            traces.at[pl.ds(0, 384)], traces.at[pl.ds(384 * (slot + 1), 384)],
            trace_send.at[slot], trace_recv.at[slot],
            device_id={"elem": other}, device_id_type=MESH,
        )

    trace_copies = [trace_copy(0, after), trace_copy(1, before)]
    for copy in trace_copies:
        copy.start()

    near = jnp.maximum(neighbour[...], 0)
    offset = lax.rem(lax.shift_right_logical(near, 4) - group + 16, 16)
    where = jnp.where(offset == 0, 0, jnp.where(offset == 1, 2, 1))
    start = where * 384 + (near & 15) * 24 + neighbour_edge[...] * 6 + flipped[...] * 5
    start = jnp.where(neighbour[...] >= 0, start, -5000).astype(jnp.float32)
    turn = (1 - 2 * flipped[...]).astype(jnp.float32)
    start = jnp.sum(exact(owner[...], start) * edge[...], axis=1, keepdims=True)
    turn = jnp.sum(exact(owner[...], turn) * edge[...], axis=1, keepdims=True)
    target = start + turn * place[...]
    source = lax.broadcasted_iota(jnp.int32, (384, 1152), 1).astype(jnp.float32)
    pick = jnp.where(source == target, 0.5, 0.0).astype(jnp.bfloat16)

    geo_column[...] = exact(pair[...], geometry[:, pl.ds(pl.multiple_of(128 * z, 128), 128)], NT)
    geo = geo_column[pl.ds(pl.multiple_of(64 * x, 64), 64), :]
    joined = jnp.where(neighbour[pl.ds(me, 1), :] >= 0, 0.5, 0.0)
    keep = 1.0 - jnp.sum(edge_own[...] * joined, axis=1, keepdims=True)
    to_x = keep * (geo[:, 0:1] * own_xi[...] + geo[:, 1:2] * own_eta[...])
    to_y = keep * (geo[:, 2:3] * own_xi[...] + geo[:, 3:4] * own_eta[...])
    gradient = split(jnp.concatenate([to_x, to_y], axis=0))

    for copy in trace_copies:
        copy.wait_recv()

    for j in range(3):
        high, low = split(traces[:, 256 * j : 256 * j + 256])
        far[:, 256 * j : 256 * j + 256] = mm(pick, high) + mm(pick, low)

    def far_part(p):
        return far.at[pl.ds(pl.multiple_of(24 * p, 8), 24)]

    def far_copy(p, slot):
        return pltpu.make_async_remote_copy(
            far_part(p), recv_far.at[slot], far_s.at[p], far_r.at[slot],
            device_id={"plane": p}, device_id_type=MESH,
        )

    def far_step(i, carry):
        far_copy(peer(i), me).start()
        return carry

    lax.fori_loop(1, 16, far_step, 0)
    recv_far[me] = far[pl.ds(pl.multiple_of(24 * me, 8), 24), :]

    def vel_wait(i, carry):
        vel_copy(peer(i), peer(i)).wait_recv()
        return carry

    lax.fori_loop(1, 16, vel_wait, 0)

    def gather(a, carry):
        lanes = pl.ds(pl.multiple_of(128 * a, 128), 128)
        for f in range(3):
            one = recv_vel[a, :, 128 * f : 128 * f + 128]
            two = recv_vel[a + 8, :, 128 * f : 128 * f + 128]
            one_z = pltpu.roll(one, 64, 1) * factor[a]
            two_z = pltpu.roll(two, 64, 1) * factor[a + 8]
            for r, (p, q) in enumerate(((one, two), (one_z, two_z))):
                rows = slice(192 * r + 64 * f, 192 * r + 64 * f + 64)
                high, low = split(p + q)
                left_high[0, rows, lanes] = high
                left_low[0, rows, lanes] = low
                high, low = split(p - q)
                left_high[1, rows, lanes] = high
                left_low[1, rows, lanes] = low
        return carry

    lax.fori_loop(0, 8, gather, 0)
    for load in loads:
        load.wait()

    total_rest[...] = jnp.zeros_like(total_rest)
    total_edge[...] = jnp.zeros_like(total_edge)

    def planes(n, carry):
        parity = n // 2
        waves = (wave_high[n], wave_low[n])
        physical = mm3((left_high[parity], left_low[parity]), waves)
        u, v, w = physical[:64], physical[64:128], physical[128:192]
        uv_edge[n, :24] = u[:24]
        uv_edge[n, 24:] = v[:24]
        for f, field in enumerate((u, v, w)):
            slopes = mm3(gradient, split(field))
            spanwise = physical[192 + 64 * f : 256 + 64 * f]
            product = u * slopes[:64] + v * slopes[64:] + w * spanwise
            own_edge[n, 24 * f : 24 * f + 24] = product[:24]
            rest[40 * f : 40 * f + 40] = product[24:]
        total_rest[parity] += mm3(split(rest[...]), waves, NT)
        return carry

    lax.fori_loop(0, 4, planes, 0)

    def combine(total, send):
        for a in range(8):
            even = total[0, :, 128 * a : 128 * a + 128]
            odd = total[1, :, 128 * a : 128 * a + 128]
            send[a] = (even + odd) * (1.0 / PLANES)
            send[a + 8] = (even - odd) * (1.0 / PLANES)

    def back_copy(send, recv, send_sem, recv_sem, p, slot):
        return pltpu.make_async_remote_copy(
            send.at[p], recv.at[slot], send_sem.at[p], recv_sem.at[slot],
            device_id={"plane": p}, device_id_type=MESH,
        )

    def back(total, send, recv, send_sem, recv_sem):
        combine(total, send)

        def step(i, carry):
            back_copy(send, recv, send_sem, recv_sem, peer(i), me).start()
            return carry

        lax.fori_loop(1, 16, step, 0)
        recv[me] = send[me]

    back(total_rest, send_rest, recv_rest, rest_s, rest_r)

    def far_wait(i, carry):
        far_copy(peer(i), peer(i)).wait_recv()
        return carry

    lax.fori_loop(1, 16, far_wait, 0)

    def gather_far(a, carry):
        lanes = pl.ds(pl.multiple_of(128 * a, 128), 128)
        for g in range(6):
            one = recv_far[a, :, 128 * g : 128 * g + 128]
            two = recv_far[a + 8, :, 128 * g : 128 * g + 128]
            left_edge[0, 24 * g : 24 * g + 24, lanes] = one + two
            left_edge[1, 24 * g : 24 * g + 24, lanes] = one - two
        return carry

    lax.fori_loop(0, 8, gather_far, 0)

    def edges(n, carry):
        parity = n // 2
        waves = (wave_high[n], wave_low[n])
        slopes = mm3(split(left_edge[parity]), waves)
        u, v = uv_edge[n, :24], uv_edge[n, 24:]
        product = jnp.concatenate(
            [
                own_edge[n, 24 * f : 24 * f + 24]
                + u * slopes[24 * f : 24 * f + 24]
                + v * slopes[72 + 24 * f : 96 + 24 * f]
                for f in range(3)
            ],
            axis=0,
        )
        total_edge[parity] += mm3(split(product), waves, NT)
        return carry

    lax.fori_loop(0, 4, edges, 0)
    back(total_edge, send_edge, recv_edge, edge_s, edge_r)

    def back_wait(recv, send, send_sem, recv_sem):
        def step(i, carry):
            back_copy(send, recv, send_sem, recv_sem, peer(i), peer(i)).wait_recv()
            return carry

        lax.fori_loop(1, 16, step, 0)

    def unpack(recv, table, add):
        def step(q, carry):
            cols = pl.ds(pl.multiple_of(128 * q, 128), 128)
            high, low = split(jnp.concatenate([recv[2 * q], recv[2 * q + 1]], axis=0))
            turned = mm(high, table[...], TN) + mm(low, table[...], TN)
            for c in range(2):
                for f in range(3):
                    part = turned[64 * c : 64 * c + 64, 128 * f : 128 * f + 128]
                    if add:
                        part = part + out[c, f, :, cols]
                    out[c, f, :, cols] = part
            return carry

        lax.fori_loop(0, 8, step, 0)

    back_wait(recv_rest, send_rest, rest_s, rest_r)
    unpack(recv_rest, unpack_rest, False)
    back_wait(recv_edge, send_edge, edge_s, edge_r)
    unpack(recv_edge, unpack_edge, True)

    def drain(i, carry):
        p = peer(i)
        vel_copy(p, me).wait_send()
        far_copy(p, me).wait_send()
        back_copy(send_rest, recv_rest, rest_s, rest_r, p, me).wait_send()
        back_copy(send_edge, recv_edge, edge_s, edge_r, p, me).wait_send()
        return carry

    lax.fori_loop(1, 16, drain, 0)
    for copy in trace_copies:
        copy.wait_send()


def shards(velocity_modes, geometry, neighbour, neighbour_edge, flipped):
    names = tables()
    constants = [jnp.asarray(value) for value in names.values()]
    vmem = pl.BlockSpec(memory_space=pltpu.VMEM)
    anywhere = pl.BlockSpec(memory_space=pl.ANY)
    f32 = jnp.float32
    return pl.pallas_call(
        kernel,
        out_shape=jax.ShapeDtypeStruct(velocity_modes.shape, f32),
        in_specs=[vmem] * (5 + len(constants) - 2) + [anywhere] * 2,
        out_specs=vmem,
        scratch_shapes=[
            pltpu.VMEM((4, 1024, 256), jnp.bfloat16),
            pltpu.VMEM((4, 1024, 256), jnp.bfloat16),
            pltpu.VMEM((128, 4), f32),
            pltpu.VMEM((8, 128, 384), f32),
            pltpu.VMEM((16, 64, 384), f32),
            pltpu.VMEM((1152, 768), f32),
            pltpu.VMEM((384, 768), f32),
            pltpu.VMEM((16, 24, 768), f32),
            pltpu.VMEM((2, 384, 1024), jnp.bfloat16),
            pltpu.VMEM((2, 384, 1024), jnp.bfloat16),
            pltpu.VMEM((2, 144, 1024), f32),
            pltpu.VMEM((120, 256), f32),
            pltpu.VMEM((4, 72, 256), f32),
            pltpu.VMEM((4, 48, 256), f32),
            pltpu.VMEM((2, 120, 1024), f32),
            pltpu.VMEM((2, 72, 1024), f32),
            pltpu.VMEM((16, 120, 128), f32),
            pltpu.VMEM((16, 120, 128), f32),
            pltpu.VMEM((16, 72, 128), f32),
            pltpu.VMEM((16, 72, 128), f32),
            pltpu.SemaphoreType.DMA((2,)),
            pltpu.SemaphoreType.DMA((2,)),
            pltpu.SemaphoreType.DMA((2,)),
        ]
        + [pltpu.SemaphoreType.DMA((16,))] * 8,
        compiler_params=pltpu.CompilerParams(
            collective_id=0, has_side_effects=True, vmem_limit_bytes=56 * 2**20
        ),
    )(velocity_modes, geometry, neighbour, neighbour_edge, flipped, *constants)


def solution(mesh):
    placed = (
        P(None, None, "plane", "elem"),
        P(None, "elem"),
        P("elem", None),
        P("elem", None),
        P("elem", None),
    )
    return jax.shard_map(
        shards,
        mesh=mesh,
        in_specs=placed,
        out_specs=P(None, None, "plane", "elem"),
        check_vma=False,
    )
```

time: 756 us -> 119 us (0.16)
  waiting for transfers between devices: 616 us -> 0 us
  Pallas kernels: 0 us -> 110 us
  local copies, waits for them, and re-layouts: 65.5 us -> 6.79 us
  other arithmetic: 38 us -> 0 us
  starting transfers between devices: 22.2 us -> 0 us
  matrix products: 8.06 us -> 0 us
    ppermute x10 -> x0, waiting for transfers between devices: 616 us -> none  [the longest x8 613 us: partner_2(): return lax.ppermute(block, axis, route)]
    pallas_call x0 -> x1, Pallas kernels: none -> 110 us  [shards(): pl.pallas_call(kernel, out_shape=jax.ShapeDtypeStruct(velocity_modes.shap...]
    scatter x4 -> x0, local copies, waits for them, and re-layouts: 29.8 us -> none  [the longest x1 9.88 us: put_edges(): return field.at[..., 1:7, 0].set(edges[..., 3, :])]
    ppermute x10 -> x0, starting transfers between devices: 22.2 us -> none  [the longest x8 20.4 us: partner_2(): return lax.ppermute(block, axis, route)]
    add x6 -> x0, other arithmetic: 12.2 us -> none  [the longest x4 10.3 us: spread_pairs(): stacked = rotate(partner + parity_sign * stacked, phase_angle)]
    another operation x8 -> x0, other arithmetic: 10.7 us -> none  [the longest x7 9.45 us: rotate(): jnp.stack([cosine * complex_pair[0] - sine_part * complex_pair[1], sine_p...]
    reshape x6 -> x0, local copies, waits for them, and re-layouts: 8.54 us -> none  [the longest x2 4.36 us: shards(): averaged.reshape(elem_dev, 4, 6, 6, planes_dev)]
    dot_general x6 -> x0, matrix products: 8.06 us -> none  [the longest x1 2.25 us: local_inverse(): jnp.einsum('bm,fmc->fbc', cosine, turned[0], precision=highest)]
  transfers between devices with their start and end apart: 10 -> 0, of which waited for: 9 -> 0; matrix products, arithmetic and copies ran while one was open for 1% -> 0% of each run, Pallas kernels for 0% -> 0%
where the time goes in v1:
time: 119 us; the launch traced here: 117 us
  Pallas kernels  110 us (92%)
  local copies, waits for them, and re-layouts  6.79 us (6%)
    pallas_call x1, Pallas kernels, shards(): pl.pallas_call(kernel, out_shape=jax.ShapeDtypeStruct(velocity_modes.shap...  110 us
    unnamed x4, local copies, waits for them, and re-layouts  6.79 us

profile of v1, /device:TPU:8, one launch (start us, length us, event | category | flops | bytes accessed | tf_op | source)
XLA Modules:
  0.0 116.8 jit_solution(4255691800168685508)
XLA Ops:
  0.0 1.4 %copy.21.neighbour = s32[16,4]{1,0:T(8,128)} copy(s32[16,4]{0,1:T(4,128)} %param.22) | data formatting | bytes 512 | tf_op args[2]
  1.4 1.4 %copy.22.neighbour_edge = s32[16,4]{1,0:T(8,128)} copy(s32[16,4]{0,1:T(4,128)} %param.23) | data formatting | bytes 512 | tf_op args[3]
  2.7 1.4 %copy.23.flipped = s32[16,4]{1,0:T(8,128)} copy(s32[16,4]{0,1:T(4,128)} %param.24) | data formatting | bytes 512 | tf_op args[4]
  4.1 110.0 %shard_map.190 = f32[2,3,64,1024]{3,2,1,0:T(8,128)} custom-call(f32[2,3,64,1024]{3,2,1,0:T(8,128)} %modes.1, f32[4,1024]{1,0:T(4,128)} %geometry.1, s32[16,4]{1,0:T(8,128)} %copy.21.neighbour, s32[16,4]{1,0:T(8,128)} %copy.22.neighbour_edge, s32[16,4]{1,0:T(8,128)} %copy.23.flipped, bf16[224,128]{1,0:T(8,128)(2,1)} %constant.30.clone.pack_high, ...), custom_call_target="tpu_custom_call" | custom-call | tf_op jit(solution)/shard_map/pallas_call | solution.py:434
  114.1 2.7 %copy.25 = f32[2,3,64,1024]{3,2,1,0:T(8,128)} copy(f32[2,3,64,1024]{3,2,1,0:T(8,128)} %shard_map.190) | data formatting | bytes 3145728

commit v2 on v1

--- a/solution.py
+++ b/solution.py
@@ -73,8 +73,7 @@
     edge_xi = np.kron(np.eye(2), xi[order[:24]])
     edge_eta = np.kron(np.eye(2), eta[order[:24]])
     pack_high, pack_low = halves(np.concatenate([pair, edge_xi, edge_eta]))
-    pack_low = pack_low[128:]
-    edge_pick = np.kron(np.eye(2), eye[:24]).astype(np.float32)
+    pack = np.concatenate([pack_high, pack_low[128:]])
 
     k = (64 * np.arange(8)[:, None] + np.arange(64)[None, :])[:, None, :]
     waves = []
@@ -82,20 +81,14 @@
         plane = 2 * (256 * (block % 2) + np.arange(256)) + block // 2
         angle = (k[..., None] * plane) % PLANES * (2.0 * np.pi / PLANES)
         waves.append(np.concatenate([np.cos(angle), -np.sin(angle)], axis=1).reshape(1024, 256))
-    wave_high, wave_low = halves(np.stack(waves))
+    wave = np.stack(halves(np.stack(waves)))
 
     mode = 64 * np.arange(16)[:, None] + np.arange(64)[None, :]
     factor = 2.0 * np.where(mode < 512, mode, mode - 1024)
-    factor = np.concatenate([-factor, factor], axis=1).astype(np.float32)[:, None, :]
-
-    own_xi = xi[order][:, order].astype(np.float32)
-    own_eta = eta[order][:, order].astype(np.float32)
-
-    row = np.arange(384)
-    owner = (row[:, None] // 24 == np.arange(16)).astype(np.float32)
-    edge = (row[:, None] % 24 // 6 == np.arange(4)).astype(np.float32)
-    place = (row % 6).astype(np.float32)[:, None]
-    edge_own = np.concatenate([edge[:24], np.zeros((40, 4), np.float32)])
+    dense = np.zeros((144, 128), np.float32)
+    dense[:64, :64] = xi[order][:, order]
+    dense[64:128, :64] = eta[order][:, order]
+    dense[128:] = np.concatenate([-factor, factor], axis=1)
 
     def unpack(points):
         out = np.zeros((2, 3, len(points), 3, 128))
@@ -105,23 +98,8 @@
                     out[side, field, r, field, 64 * side + point] = 1.0
         return out.reshape(6 * len(points), 384).astype(ml_dtypes.bfloat16)
 
-    return dict(
-        pack_high=pack_high,
-        pack_low=pack_low,
-        edge_pick=edge_pick,
-        pair=pair.astype(np.float32),
-        factor=factor,
-        own_xi=own_xi,
-        own_eta=own_eta,
-        owner=owner,
-        edge=edge,
-        place=place,
-        edge_own=edge_own,
-        unpack_edge=unpack(order[:24]),
-        unpack_rest=unpack(order[24:]),
-        wave_high=wave_high,
-        wave_low=wave_low,
-    )
+    turn = np.concatenate([unpack(order[:24]), unpack(order[24:])])
+    return pack, dense, turn, wave
 
 
 def split(x):
@@ -148,13 +126,14 @@
 
 
 def kernel(
-    modes, geometry, neighbour, neighbour_edge, flipped,
-    pack_high, pack_low, edge_pick, pair, factor, own_xi, own_eta, owner, edge, place, edge_own,
-    unpack_edge, unpack_rest, wave_high_hbm, wave_low_hbm,
-    out,
-    wave_high, wave_low, geo_column, send_vel, recv_vel, traces, far, recv_far, left_high, left_low,
+    modes_hbm, geometry_hbm, neighbour_hbm, neighbour_edge_hbm, flipped_hbm,
+    pack_hbm, dense_hbm, turn_hbm, wave_hbm,
+    out_hbm,
+    modes, geometry, neighbour, neighbour_edge, flipped, pack_table, dense, turn_table, wave, out,
+    geo_column, send_vel, recv_vel, traces, far, recv_far, left_high, left_low,
     left_edge, rest, own_edge, uv_edge, total_rest, total_edge, send_rest, recv_rest, send_edge, recv_edge,
-    wave_sem, trace_send, trace_recv, vel_s, vel_r, far_s, far_r, rest_s, rest_r, edge_s, edge_r,
+    load_sem, mode_sem, out_sem,
+    trace_send, trace_recv, vel_s, vel_r, far_s, far_r, rest_s, rest_r, edge_s, edge_r,
 ):
     me = lax.axis_index("plane")
     group = lax.axis_index("elem")
@@ -166,13 +145,6 @@
         dz = (h + 1) // 2 * (2 * (h % 2) - 1)
         return (z + dz + 8) % 8 * 2 + (x + i) % 2
 
-    loads = [
-        pltpu.make_async_copy(wave_high_hbm, wave_high, wave_sem.at[0]),
-        pltpu.make_async_copy(wave_low_hbm, wave_low, wave_sem.at[1]),
-    ]
-    for load in loads:
-        load.start()
-
     barrier = pltpu.get_barrier_semaphore()
 
     def greet(i, carry):
@@ -184,18 +156,48 @@
     after = (group + 1) % 16
     for other in (before, after):
         pl.semaphore_signal(barrier, inc=1, device_id={"elem": other}, device_id_type=MESH)
-    pl.semaphore_wait(barrier, 17)
+
+    def pair_cols(q):
+        return pl.ds(pl.multiple_of(128 * q, 128), 128)
+
+    def mode_load(q):
+        return pltpu.make_async_copy(modes_hbm.at[:, :, :, pair_cols(q)], modes.at[q], mode_sem.at[q])
+
+    loads = [
+        pltpu.make_async_copy(source, target, load_sem.at[i])
+        for i, (source, target) in enumerate((
+            (pack_hbm, pack_table),
+            (geometry_hbm, geometry),
+            (neighbour_hbm, neighbour),
+            (neighbour_edge_hbm, neighbour_edge),
+            (flipped_hbm, flipped),
+            (dense_hbm, dense),
+            (wave_hbm, wave),
+            (turn_hbm, turn_table),
+        ))
+    ]
+    loads[0].start()
+    mode_load(peer(2) // 2).start()
+    loads[1].start()
+
+    def mode_start(h, carry):
+        mode_load(peer(2 * h) // 2).start()
+        return carry
+
+    lax.fori_loop(2, 8, mode_start, 0)
+    mode_load(z).start()
+    for load in loads[2:]:
+        load.start()
 
     def pack(q):
-        cols = pl.ds(pl.multiple_of(128 * q, 128), 128)
-        block = jnp.concatenate(
-            [modes[c, f, :, cols] for f in range(3) for c in range(2)], axis=0
-        )
+        mode_load(q).wait()
+        block = jnp.concatenate([modes[q, c, f] for f in range(3) for c in range(2)], axis=0)
         high, low = split(block)
-        both = mm(pack_high[...], high, NT) + mm(pack_high[...], low, NT)
+        both = mm(pack_table[:224], high, NT) + mm(pack_table[:224], low, NT)
         send_vel[q] = both[:128]
-        along = both[128:] + mm(pack_low[...], high, NT)
-        geo = exact(edge_pick[...], geometry[:, cols], NT)
+        along = both[128:] + mm(pack_table[224:], high, NT)
+        pick = jnp.concatenate([pack_table[:24], pack_table[64:88]], axis=0).astype(jnp.float32)
+        geo = exact(pick, geometry[:, pair_cols(q)], NT)
         rows = pl.ds(pl.multiple_of(48 * q, 16), 48)
         traces[rows, :384] = geo[:, 0:1] * along[:48] + geo[:, 1:2] * along[48:]
         traces[rows, 384:] = geo[:, 2:3] * along[:48] + geo[:, 3:4] * along[48:]
@@ -209,9 +211,12 @@
             device_id={"plane": p}, device_id_type=MESH,
         )
 
-    pack(z)
-    vel_copy(peer(1), me).start()
-    recv_vel[me] = send_vel[z, pl.ds(pl.multiple_of(x * 64, 64), 64), :]
+    loads[0].wait()
+    loads[1].wait()
+    pack(peer(2) // 2)
+    pl.semaphore_wait(barrier, 17)
+    vel_copy(peer(2), me).start()
+    vel_copy(peer(3), me).start()
 
     def pack_step(h, carry):
         pack(peer(2 * h) // 2)
@@ -219,7 +224,10 @@
         vel_copy(peer(2 * h + 1), me).start()
         return carry
 
-    lax.fori_loop(1, 8, pack_step, 0)
+    lax.fori_loop(2, 8, pack_step, 0)
+    pack(z)
+    vel_copy(peer(1), me).start()
+    recv_vel[me] = send_vel[z, pl.ds(pl.multiple_of(x * 64, 64), 64), :]
 
     def trace_copy(slot, other):
         return pltpu.make_async_remote_copy(
@@ -232,24 +240,43 @@
     for copy in trace_copies:
         copy.start()
 
+    for load in loads[2:6]:
+        load.wait()
+
+    def iota(shape, axis):
+        return lax.broadcasted_iota(jnp.int32, shape, axis)
+
+    def rows_of(shape):
+        row = iota(shape, 0)
+        element = (row * 2731) >> 16
+        edge = ((row - element * 24) * 10923) >> 16
+        return element, edge, row - element * 24 - edge * 6
+
     near = jnp.maximum(neighbour[...], 0)
-    offset = lax.rem(lax.shift_right_logical(near, 4) - group + 16, 16)
+    offset = ((near >> 4) - group + 16) & 15
     where = jnp.where(offset == 0, 0, jnp.where(offset == 1, 2, 1))
     start = where * 384 + (near & 15) * 24 + neighbour_edge[...] * 6 + flipped[...] * 5
     start = jnp.where(neighbour[...] >= 0, start, -5000).astype(jnp.float32)
     turn = (1 - 2 * flipped[...]).astype(jnp.float32)
-    start = jnp.sum(exact(owner[...], start) * edge[...], axis=1, keepdims=True)
-    turn = jnp.sum(exact(owner[...], turn) * edge[...], axis=1, keepdims=True)
-    target = start + turn * place[...]
-    source = lax.broadcasted_iota(jnp.int32, (384, 1152), 1).astype(jnp.float32)
-    pick = jnp.where(source == target, 0.5, 0.0).astype(jnp.bfloat16)
-
-    geo_column[...] = exact(pair[...], geometry[:, pl.ds(pl.multiple_of(128 * z, 128), 128)], NT)
+    owner = (rows_of((384, 16))[0] == iota((384, 16), 1)).astype(jnp.float32)
+    edge = (rows_of((384, 4))[1] == iota((384, 4), 1)).astype(jnp.float32)
+    place = rows_of((384, 1))[2].astype(jnp.float32)
+    start = jnp.sum(exact(owner, start, NT) * edge, axis=1, keepdims=True)
+    turn = jnp.sum(exact(owner, turn, NT) * edge, axis=1, keepdims=True)
+    target = start + turn * place
+    pick = jnp.where(iota((384, 1152), 1).astype(jnp.float32) == target, 0.5, 0.0)
+    pick = pick.astype(jnp.bfloat16)
+
+    geo_column[...] = exact(pack_table[:128].astype(jnp.float32), geometry[:, pair_cols(z)], NT)
     geo = geo_column[pl.ds(pl.multiple_of(64 * x, 64), 64), :]
-    joined = jnp.where(neighbour[pl.ds(me, 1), :] >= 0, 0.5, 0.0)
-    keep = 1.0 - jnp.sum(edge_own[...] * joined, axis=1, keepdims=True)
-    to_x = keep * (geo[:, 0:1] * own_xi[...] + geo[:, 1:2] * own_eta[...])
-    to_y = keep * (geo[:, 2:3] * own_xi[...] + geo[:, 3:4] * own_eta[...])
+    joined = jnp.where(neighbour[...] >= 0, 0.5, 0.0)
+    edge_own = (rows_of((64, 4))[1] + 4 * rows_of((64, 4))[0] == iota((64, 4), 1))
+    joined = exact(edge_own.astype(jnp.float32), joined)
+    joined = jnp.where(iota((64, 16), 1) == me, joined, 0.0)
+    keep = 1.0 - jnp.sum(joined, axis=1, keepdims=True)
+    own_xi, own_eta = dense[:64, :64], dense[64:128, :64]
+    to_x = keep * (geo[:, 0:1] * own_xi + geo[:, 1:2] * own_eta)
+    to_y = keep * (geo[:, 2:3] * own_xi + geo[:, 3:4] * own_eta)
     gradient = split(jnp.concatenate([to_x, to_y], axis=0))
 
     for copy in trace_copies:
@@ -286,8 +313,8 @@
         for f in range(3):
             one = recv_vel[a, :, 128 * f : 128 * f + 128]
             two = recv_vel[a + 8, :, 128 * f : 128 * f + 128]
-            one_z = pltpu.roll(one, 64, 1) * factor[a]
-            two_z = pltpu.roll(two, 64, 1) * factor[a + 8]
+            one_z = pltpu.roll(one, 64, 1) * dense[pl.ds(128 + a, 1), :]
+            two_z = pltpu.roll(two, 64, 1) * dense[pl.ds(136 + a, 1), :]
             for r, (p, q) in enumerate(((one, two), (one_z, two_z))):
                 rows = slice(192 * r + 64 * f, 192 * r + 64 * f + 64)
                 high, low = split(p + q)
@@ -299,7 +326,7 @@
         return carry
 
     lax.fori_loop(0, 8, gather, 0)
-    for load in loads:
+    for load in loads[6:]:
         load.wait()
 
     total_rest[...] = jnp.zeros_like(total_rest)
@@ -307,7 +334,7 @@
 
     def planes(n, carry):
         parity = n // 2
-        waves = (wave_high[n], wave_low[n])
+        waves = (wave[0, n], wave[1, n])
         physical = mm3((left_high[parity], left_low[parity]), waves)
         u, v, w = physical[:64], physical[64:128], physical[128:192]
         uv_edge[n, :24] = u[:24]
@@ -367,7 +394,7 @@
 
     def edges(n, carry):
         parity = n // 2
-        waves = (wave_high[n], wave_low[n])
+        waves = (wave[0, n], wave[1, n])
         slopes = mm3(split(left_edge[parity]), waves)
         u, v = uv_edge[n, :24], uv_edge[n, 24:]
         product = jnp.concatenate(
@@ -385,32 +412,37 @@
     lax.fori_loop(0, 4, edges, 0)
     back(total_edge, send_edge, recv_edge, edge_s, edge_r)
 
-    def back_wait(recv, send, send_sem, recv_sem):
-        def step(i, carry):
+    def out_copy(q):
+        return pltpu.make_async_copy(out.at[q], out_hbm.at[:, :, :, pair_cols(q)], out_sem.at[q])
+
+    def unpack(q, recv, rows, add):
+        high, low = split(jnp.concatenate([recv[2 * q], recv[2 * q + 1]], axis=0))
+        turned = mm(high, turn_table[rows], TN) + mm(low, turn_table[rows], TN)
+        for c in range(2):
+            for f in range(3):
+                part = turned[64 * c : 64 * c + 64, 128 * f : 128 * f + 128]
+                if add:
+                    part = part + out[q, c, f]
+                out[q, c, f] = part
+        if add:
+            out_copy(q).start()
+
+    def unpack_all(send, recv, send_sem, recv_sem, rows, add):
+        def arrive(i):
             back_copy(send, recv, send_sem, recv_sem, peer(i), peer(i)).wait_recv()
+
+        def step(h, carry):
+            arrive(2 * h)
+            arrive(2 * h + 1)
+            unpack(peer(2 * h) // 2, recv, rows, add)
             return carry
 
-        lax.fori_loop(1, 16, step, 0)
-
-    def unpack(recv, table, add):
-        def step(q, carry):
-            cols = pl.ds(pl.multiple_of(128 * q, 128), 128)
-            high, low = split(jnp.concatenate([recv[2 * q], recv[2 * q + 1]], axis=0))
-            turned = mm(high, table[...], TN) + mm(low, table[...], TN)
-            for c in range(2):
-                for f in range(3):
-                    part = turned[64 * c : 64 * c + 64, 128 * f : 128 * f + 128]
-                    if add:
-                        part = part + out[c, f, :, cols]
-                    out[c, f, :, cols] = part
-            return carry
-
-        lax.fori_loop(0, 8, step, 0)
-
-    back_wait(recv_rest, send_rest, rest_s, rest_r)
-    unpack(recv_rest, unpack_rest, False)
-    back_wait(recv_edge, send_edge, edge_s, edge_r)
-    unpack(recv_edge, unpack_edge, True)
+        arrive(1)
+        unpack(z, recv, rows, add)
+        lax.fori_loop(1, 8, step, 0)
+
+    unpack_all(send_rest, recv_rest, rest_s, rest_r, slice(144, 384), False)
+    unpack_all(send_edge, recv_edge, edge_s, edge_r, slice(0, 144), True)
 
     def drain(i, carry):
         p = peer(i)
@@ -423,22 +455,26 @@
     lax.fori_loop(1, 16, drain, 0)
     for copy in trace_copies:
         copy.wait_send()
+    for q in range(8):
+        out_copy(q).wait()
 
 
 def shards(velocity_modes, geometry, neighbour, neighbour_edge, flipped):
-    names = tables()
-    constants = [jnp.asarray(value) for value in names.values()]
-    vmem = pl.BlockSpec(memory_space=pltpu.VMEM)
+    constants = [jnp.asarray(value) for value in tables()]
     anywhere = pl.BlockSpec(memory_space=pl.ANY)
     f32 = jnp.float32
+    operands = (velocity_modes, geometry, neighbour.T, neighbour_edge.T, flipped.T, *constants)
     return pl.pallas_call(
         kernel,
         out_shape=jax.ShapeDtypeStruct(velocity_modes.shape, f32),
-        in_specs=[vmem] * (5 + len(constants) - 2) + [anywhere] * 2,
-        out_specs=vmem,
+        in_specs=[anywhere] * len(operands),
+        out_specs=anywhere,
         scratch_shapes=[
-            pltpu.VMEM((4, 1024, 256), jnp.bfloat16),
-            pltpu.VMEM((4, 1024, 256), jnp.bfloat16),
+            pltpu.VMEM((8, 2, 3, 64, 128), f32),
+        ]
+        + [pltpu.VMEM(value.shape, value.dtype) for value in operands[1:]]
+        + [
+            pltpu.VMEM((8, 2, 3, 64, 128), f32),
             pltpu.VMEM((128, 4), f32),
             pltpu.VMEM((8, 128, 384), f32),
             pltpu.VMEM((16, 64, 384), f32),
@@ -457,7 +493,9 @@
             pltpu.VMEM((16, 120, 128), f32),
             pltpu.VMEM((16, 72, 128), f32),
             pltpu.VMEM((16, 72, 128), f32),
-            pltpu.SemaphoreType.DMA((2,)),
+            pltpu.SemaphoreType.DMA((8,)),
+            pltpu.SemaphoreType.DMA((8,)),
+            pltpu.SemaphoreType.DMA((8,)),
             pltpu.SemaphoreType.DMA((2,)),
             pltpu.SemaphoreType.DMA((2,)),
         ]
@@ -465,7 +503,7 @@
         compiler_params=pltpu.CompilerParams(
             collective_id=0, has_side_effects=True, vmem_limit_bytes=56 * 2**20
         ),
-    )(velocity_modes, geometry, neighbour, neighbour_edge, flipped, *constants)
+    )(*operands)
 
 
 def solution(mesh):

time: 119 us -> 109 us (0.916)
  Pallas kernels: 110 us -> 105 us
  local copies, waits for them, and re-layouts: 6.79 us -> 2.73 us
    pallas_call x1, Pallas kernels: 110 us -> 105 us  [shards(): pl.pallas_call(kernel, out_shape=jax.ShapeDtypeStruct(velocity_modes.shap...]
    unnamed x4 -> x1, local copies, waits for them, and re-layouts: 6.79 us -> 2.73 us
where the time goes in v2:
time: 109 us; the launch traced here: 107 us
  Pallas kernels  105 us (96%)
  local copies, waits for them, and re-layouts  2.73 us (3%)
    pallas_call x1, Pallas kernels, shards(): pl.pallas_call(kernel, out_shape=jax.ShapeDtypeStruct(velocity_modes.shap...  105 us
    unnamed x1, local copies, waits for them, and re-layouts  2.73 us

profile of v2, /device:TPU:8, one launch (start us, length us, event | category | flops | bytes accessed | tf_op | source)
XLA Modules:
  0.0 107.5 jit_solution(11001893444602321574)
XLA Ops:
  0.0 104.8 %shard_map.91 = f32[2,3,64,1024]{3,2,1,0:T(8,128)} custom-call(f32[2,3,64,1024]{3,2,1,0:T(8,128)} %modes_hbm.1, f32[4,1024]{1,0:T(4,128)} %geometry_hbm.1, s32[4,16]{1,0:T(4,128)} %bitcast.3, s32[4,16]{1,0:T(4,128)} %bitcast.4, s32[4,16]{1,0:T(4,128)} %bitcast.5, bf16[320,128]{1,0:T(8,128)(2,1)} %constant.8.clone.pack_hbm, ...), custom_call_target="tpu_custom_call" | custom-call | tf_op jit(solution)/shard_map/pallas_call | solution.py:467
  104.8 2.7 %copy.11 = f32[2,3,64,1024]{3,2,1,0:T(8,128)} copy(f32[2,3,64,1024]{3,2,1,0:T(8,128)} %shard_map.91) | data formatting | bytes 3145728

commit v3 on v2

--- a/solution.py
+++ b/solution.py
@@ -9,6 +9,7 @@
 
 PLANES = 1024
 POINTS = 64
+LEADER, CLERK = 2, 3
 MESH = pl.DeviceIdType.MESH
 highest = lax.Precision.HIGHEST
 gll_nodes = [
@@ -132,7 +133,7 @@
     modes, geometry, neighbour, neighbour_edge, flipped, pack_table, dense, turn_table, wave, out,
     geo_column, send_vel, recv_vel, traces, far, recv_far, left_high, left_low,
     left_edge, rest, own_edge, uv_edge, total_rest, total_edge, send_rest, recv_rest, send_edge, recv_edge,
-    load_sem, mode_sem, out_sem,
+    plane_ok, elem_ok, load_sem, mode_sem, out_sem,
     trace_send, trace_recv, vel_s, vel_r, far_s, far_r, rest_s, rest_r, edge_s, edge_r,
 ):
     me = lax.axis_index("plane")
@@ -146,16 +147,51 @@
         return (z + dz + 8) % 8 * 2 + (x + i) % 2
 
     barrier = pltpu.get_barrier_semaphore()
-
-    def greet(i, carry):
-        pl.semaphore_signal(barrier, inc=1, device_id={"plane": peer(i)}, device_id_type=MESH)
-        return carry
-
-    lax.fori_loop(1, 16, greet, 0)
     before = (group + 15) % 16
     after = (group + 1) % 16
+
+    def greet(i, carry):
+        @pl.when(peer(i) != CLERK)
+        def _():
+            pl.semaphore_signal(barrier, inc=1, device_id={"plane": peer(i)}, device_id_type=MESH)
+
+        return carry
+
+    lax.fori_loop(1, 16, greet, 0)
     for other in (before, after):
-        pl.semaphore_signal(barrier, inc=1, device_id={"elem": other}, device_id_type=MESH)
+        pl.semaphore_signal(
+            barrier, inc=1, device_id={"plane": CLERK, "elem": other}, device_id_type=MESH
+        )
+
+    def enter_plane():
+        @pl.when(me != CLERK)
+        def _():
+            pl.semaphore_wait(barrier, 15)
+
+        @pl.when(me == LEADER)
+        def _():
+            pl.semaphore_signal(plane_ok, inc=1, device_id={"plane": CLERK}, device_id_type=MESH)
+
+        @pl.when(me == CLERK)
+        def _():
+            pl.semaphore_wait(plane_ok, 1)
+
+    def enter_elem():
+        @pl.when(me == CLERK)
+        def _():
+            pl.semaphore_wait(barrier, 32)
+
+            def tell(i, carry):
+                pl.semaphore_signal(
+                    elem_ok, inc=1, device_id={"plane": peer(i)}, device_id_type=MESH
+                )
+                return carry
+
+            lax.fori_loop(1, 16, tell, 0)
+
+        @pl.when(me != CLERK)
+        def _():
+            pl.semaphore_wait(elem_ok, 1)
 
     def pair_cols(q):
         return pl.ds(pl.multiple_of(128 * q, 128), 128)
@@ -214,7 +250,7 @@
     loads[0].wait()
     loads[1].wait()
     pack(peer(2) // 2)
-    pl.semaphore_wait(barrier, 17)
+    enter_plane()
     vel_copy(peer(2), me).start()
     vel_copy(peer(3), me).start()
 
@@ -228,6 +264,8 @@
     pack(z)
     vel_copy(peer(1), me).start()
     recv_vel[me] = send_vel[z, pl.ds(pl.multiple_of(x * 64, 64), 64), :]
+
+    enter_elem()
 
     def trace_copy(slot, other):
         return pltpu.make_async_remote_copy(
@@ -493,6 +531,8 @@
             pltpu.VMEM((16, 120, 128), f32),
             pltpu.VMEM((16, 72, 128), f32),
             pltpu.VMEM((16, 72, 128), f32),
+            pltpu.SemaphoreType.REGULAR,
+            pltpu.SemaphoreType.REGULAR,
             pltpu.SemaphoreType.DMA((8,)),
             pltpu.SemaphoreType.DMA((8,)),
             pltpu.SemaphoreType.DMA((8,)),

time: 109 us -> 108 us (level); the launches traced: 107 us -> 108 us
  no operation moved by 1% of the time
where the time goes in v3:
time: 108 us
  Pallas kernels  105 us (97%)
  local copies, waits for them, and re-layouts  2.73 us (3%)
    pallas_call x1, Pallas kernels, shards(): pl.pallas_call(kernel, out_shape=jax.ShapeDtypeStruct(velocity_modes.shap...  105 us
    unnamed x1, local copies, waits for them, and re-layouts  2.73 us

profile of v3, /device:TPU:8, one launch (start us, length us, event | category | flops | bytes accessed | tf_op | source)
XLA Modules:
  0.0 107.7 jit_solution(12406858102840660490)
XLA Ops:
  0.0 105.0 %shard_map.91 = f32[2,3,64,1024]{3,2,1,0:T(8,128)} custom-call(f32[2,3,64,1024]{3,2,1,0:T(8,128)} %modes_hbm.1, f32[4,1024]{1,0:T(4,128)} %geometry_hbm.1, s32[4,16]{1,0:T(4,128)} %bitcast.3, s32[4,16]{1,0:T(4,128)} %bitcast.4, s32[4,16]{1,0:T(4,128)} %bitcast.5, bf16[320,128]{1,0:T(8,128)(2,1)} %constant.8.clone.pack_hbm, ...), custom_call_target="tpu_custom_call" | custom-call | tf_op jit(solution)/shard_map/pallas_call | solution.py:505
  105.0 2.7 %copy.11 = f32[2,3,64,1024]{3,2,1,0:T(8,128)} copy(f32[2,3,64,1024]{3,2,1,0:T(8,128)} %shard_map.91) | data formatting | bytes 3145728

commit v4 on v3

v4 whole, which is shorter than its diff:
```python
import jax
import jax.numpy as jnp
import ml_dtypes
import numpy as np
from jax import lax
from jax.experimental import pallas as pl
from jax.experimental.pallas import tpu as pltpu
from jax.sharding import PartitionSpec as P

PLANES = 1024
POINTS = 64
LEADER, CLERK = 2, 3
EARLY, MIDDLE = 16, 12
FIRST = 64
MESH = pl.DeviceIdType.MESH
highest = lax.Precision.HIGHEST
gll_nodes = [
    -1.0,
    -0.8717401485096066,
    -0.5917001814331423,
    -0.2092992179024789,
    0.2092992179024789,
    0.5917001814331423,
    0.8717401485096066,
    1.0,
]


def legendre_seven(point_value):
    earlier_value = 1.0
    current_value = point_value
    for degree_index in range(1, 7):
        next_value = (
            (2 * degree_index + 1) * point_value * current_value - degree_index * earlier_value
        ) / (degree_index + 1)
        earlier_value = current_value
        current_value = next_value
    return current_value


def gll_matrices():
    legendre_vals = [legendre_seven(node_value) for node_value in gll_nodes]
    deriv_matrix = np.zeros((8, 8))
    for row_index in range(8):
        for col_index in range(8):
            if row_index != col_index:
                deriv_matrix[row_index, col_index] = (
                    legendre_vals[row_index]
                    / legendre_vals[col_index]
                    / (gll_nodes[row_index] - gll_nodes[col_index])
                )
    deriv_matrix[0, 0] = -14.0
    deriv_matrix[7, 7] = 14.0
    identity = np.eye(8)
    return (np.kron(identity, deriv_matrix), np.kron(deriv_matrix, identity))


def halves(matrix):
    high = matrix.astype(ml_dtypes.bfloat16)
    low = (matrix - high.astype(np.float64)).astype(ml_dtypes.bfloat16)
    return high, low


def point_order():
    steps = range(1, 7)
    order = [p for p in steps] + [8 * p + 7 for p in steps]
    order += [56 + p for p in steps] + [8 * p for p in steps]
    return order + [r for r in range(POINTS) if r not in order]


def tables():
    order = point_order()
    xi, eta = gll_matrices()
    pair = np.kron(np.eye(2), np.eye(POINTS)[order]).astype(ml_dtypes.bfloat16)

    k = (64 * np.arange(8)[:, None] + np.arange(64)[None, :])[:, None, :]
    waves = []
    for block in range(4):
        plane = 2 * (256 * (block % 2) + np.arange(256)) + block // 2
        angle = (k[..., None] * plane) % PLANES * (2.0 * np.pi / PLANES)
        waves.append(np.concatenate([np.cos(angle), -np.sin(angle)], axis=1).reshape(1024, 256))
    wave = np.stack(halves(np.stack(waves)))

    mode = 64 * np.arange(16)[:, None] + np.arange(64)[None, :]
    factor = 2.0 * np.where(mode < 512, mode, mode - 1024)
    dense = np.zeros((144, 128), np.float32)
    dense[:64, :64] = xi[order][:, order]
    dense[64:128, :64] = eta[order][:, order]
    dense[128:] = np.concatenate([-factor, factor], axis=1)
    return pair, dense, wave, np.ascontiguousarray(wave.transpose(0, 1, 3, 2))


def split(x):
    high = x.astype(jnp.bfloat16)
    return high, (x - high.astype(jnp.float32)).astype(jnp.bfloat16)


def mm(a, b, dims=((1,), (0,))):
    return lax.dot_general(a, b, (dims, ((), ())), preferred_element_type=jnp.float32)


NT = ((1,), (1,))
TN = ((0,), (0,))


def mm3(a, b, dims=((1,), (0,))):
    return mm(a[0], b[0], dims) + (mm(a[0], b[1], dims) + mm(a[1], b[0], dims))


def exact(a, b, dims=((1,), (0,))):
    return lax.dot_general(
        a, b, (dims, ((), ())), precision=highest, preferred_element_type=jnp.float32
    )


def kernel(
    modes_hbm, geometry_hbm, neighbour_hbm, neighbour_edge_hbm, flipped_hbm,
    pair_hbm, dense_hbm, wave_hbm, back_wave_hbm,
    out_hbm,
    modes, geometry, neighbour, neighbour_edge, flipped, pair, dense, wave, back_wave, out,
    geo_column, send_vel, recv_vel, traces, far, recv_far, left_high, left_low, physical,
    left_far, far_modes, slopes_edge, product, total, total_far, send_main, recv_main, send_far, shares, added,
    plane_ok, elem_ok, load_sem, mode_sem, out_sem,
    trace_send, trace_recv, share_send, share_recv, vel_s, vel_r, far_s, far_r, main_s, main_r, back_s, back_r,
):
    me = lax.axis_index("plane")
    group = lax.axis_index("elem")
    z = me // 2
    x = me % 2

    def peer(i):
        h = i // 2
        dz = (h + 1) // 2 * (2 * (h % 2) - 1)
        return (z + dz + 8) % 8 * 2 + (x + i) % 2

    barrier = pltpu.get_barrier_semaphore()
    before = (group + 15) % 16
    after = (group + 1) % 16

    def greet(i, carry):
        @pl.when(peer(i) != CLERK)
        def _():
            pl.semaphore_signal(barrier, inc=1, device_id={"plane": peer(i)}, device_id_type=MESH)

        return carry

    lax.fori_loop(1, 16, greet, 0)
    for other in (before, after):
        pl.semaphore_signal(
            barrier, inc=1, device_id={"plane": CLERK, "elem": other}, device_id_type=MESH
        )

    def enter_plane():
        @pl.when(me != CLERK)
        def _():
            pl.semaphore_wait(barrier, 15)

        @pl.when(me == LEADER)
        def _():
            pl.semaphore_signal(plane_ok, inc=1, device_id={"plane": CLERK}, device_id_type=MESH)

        @pl.when(me == CLERK)
        def _():
            pl.semaphore_wait(plane_ok, 1)

    def enter_elem():
        @pl.when(me == CLERK)
        def _():
            pl.semaphore_wait(barrier, 32)

            def tell(i, carry):
                pl.semaphore_signal(
                    elem_ok, inc=1, device_id={"plane": peer(i)}, device_id_type=MESH
                )
                return carry

            lax.fori_loop(1, 16, tell, 0)

        @pl.when(me != CLERK)
        def _():
            pl.semaphore_wait(elem_ok, 1)

    def pair_cols(q):
        return pl.ds(pl.multiple_of(128 * q, 128), 128)

    def mode_load(q):
        return pltpu.make_async_copy(modes_hbm.at[:, :, :, pair_cols(q)], modes.at[q], mode_sem.at[q])

    loads = [
        pltpu.make_async_copy(source, target, load_sem.at[i])
        for i, (source, target) in enumerate((
            (pair_hbm, pair),
            (geometry_hbm, geometry),
            (neighbour_hbm, neighbour),
            (neighbour_edge_hbm, neighbour_edge),
            (flipped_hbm, flipped),
            (dense_hbm, dense),
            (wave_hbm, wave),
            (back_wave_hbm, back_wave),
        ))
    ]
    loads[0].start()
    mode_load(peer(2) // 2).start()
    loads[1].start()

    def mode_start(h, carry):
        mode_load(peer(2 * h) // 2).start()
        return carry

    lax.fori_loop(2, 8, mode_start, 0)
    mode_load(z).start()
    for load in loads[2:]:
        load.start()

    def pack(q):
        mode_load(q).wait()
        block = jnp.concatenate([modes[q, c, f] for f in range(3) for c in range(2)], axis=0)
        high, low = split(block)
        send_vel[q] = mm(pair[...], high, NT) + mm(pair[...], low, NT)

    def vel_part(p):
        return send_vel.at[p // 2, pl.ds(pl.multiple_of(p % 2 * 64, 64), 64)]

    def vel_copy(p, slot):
        return pltpu.make_async_remote_copy(
            vel_part(p), recv_vel.at[slot], vel_s.at[p], vel_r.at[slot],
            device_id={"plane": p}, device_id_type=MESH,
        )

    loads[0].wait()
    pack(peer(2) // 2)
    enter_plane()
    vel_copy(peer(2), me).start()
    vel_copy(peer(3), me).start()

    def pack_step(h, carry):
        pack(peer(2 * h) // 2)
        vel_copy(peer(2 * h), me).start()
        vel_copy(peer(2 * h + 1), me).start()
        return carry

    lax.fori_loop(2, 8, pack_step, 0)
    pack(z)
    vel_copy(peer(1), me).start()
    recv_vel[me] = send_vel[z, pl.ds(pl.multiple_of(x * 64, 64), 64), :]

    for load in loads[1:6]:
        load.wait()

    def iota(shape, axis):
        return lax.broadcasted_iota(jnp.int32, shape, axis)

    def rows_of(shape):
        row = iota(shape, 0)
        element = (row * 2731) >> 16
        edge = ((row - element * 24) * 10923) >> 16
        return element, edge, row - element * 24 - edge * 6

    owner = (rows_of((384, 16))[0] == iota((384, 16), 1)).astype(jnp.float32)
    edge = (rows_of((384, 4))[1] == iota((384, 4), 1)).astype(jnp.float32)

    def per_row(table):
        return jnp.sum(exact(owner, table, NT) * edge, axis=1, keepdims=True)

    def one_hot(width, target):
        return iota((384, width), 1).astype(jnp.float32) == target

    near = jnp.maximum(neighbour[...], 0)
    offset = ((near >> 4) - group + 16) & 15
    where = jnp.where(offset == 0, 0, jnp.where(offset == 1, 2, 1))
    start = where * 384 + (near & 15) * 24 + neighbour_edge[...] * 6
    start = per_row(jnp.where(neighbour[...] >= 0, start, -5000).astype(jnp.float32))
    place = rows_of((384, 1))[2].astype(jnp.float32)
    turned = per_row(flipped[...].astype(jnp.float32))
    turned = place + turned * (5.0 - 2.0 * place)
    row = iota((384, 1), 0).astype(jnp.float32)
    turn = jnp.where(one_hot(384, row - place + turned), 1.0, 0.0).astype(jnp.bfloat16)

    for e in range(16):
        left_far[24 * e : 24 * e + 24] = send_vel[e // 2, 64 * (e % 2) : 64 * (e % 2) + 24, :256]
    high, low = split(left_far[...])
    traces[:384] = mm(turn, high) + mm(turn, low)

    enter_elem()

    def swap(array, width, send_sem, recv_sem):
        copies = [
            pltpu.make_async_remote_copy(
                array.at[pl.ds(0, 384)], array.at[pl.ds(384 * (slot + 1), 384)],
                send_sem.at[slot], recv_sem.at[slot],
                device_id={"elem": other}, device_id_type=MESH,
            )
            for slot, other in ((0, after), (1, before))
        ]
        for copy in copies:
            copy.start()
        return copies

    trace_copies = swap(traces, 256, trace_send, trace_recv)
    pick = jnp.where(one_hot(1152, start + place), 1.0, 0.0).astype(jnp.bfloat16)

    geo_column[...] = exact(pair[...].astype(jnp.float32), geometry[:, pair_cols(z)], NT)
    geo = geo_column[pl.ds(pl.multiple_of(64 * x, 64), 64), :]
    joined = jnp.where(neighbour[...] >= 0, 0.5, 0.0)
    edge_own = rows_of((64, 4))[1] + 4 * rows_of((64, 4))[0] == iota((64, 4), 1)
    joined = exact(edge_own.astype(jnp.float32), joined)
    joined = jnp.where(iota((64, 16), 1) == me, joined, 0.0)
    keep = 1.0 - jnp.sum(joined, axis=1, keepdims=True)
    own_xi, own_eta = dense[:64, :64], dense[64:128, :64]
    to_x = geo[:, 0:1] * own_xi + geo[:, 1:2] * own_eta
    to_y = geo[:, 2:3] * own_xi + geo[:, 3:4] * own_eta
    gradient = split(jnp.concatenate([to_x, to_y], axis=0))

    for copy in trace_copies:
        copy.wait_recv()
    high, low = split(traces[...])
    far[...] = mm(pick, high) + mm(pick, low)

    def far_part(p):
        return far.at[pl.ds(pl.multiple_of(24 * p, 8), 24)]

    def far_copy(p, slot):
        return pltpu.make_async_remote_copy(
            far_part(p), recv_far.at[slot], far_s.at[p], far_r.at[slot],
            device_id={"plane": p}, device_id_type=MESH,
        )

    def loop(low, high, body):
        def step(i, carry):
            body(i)
            return carry

        lax.fori_loop(low, high, step, 0)

    loop(2, EARLY, lambda i: vel_copy(peer(i), me).wait_send())
    loop(1, 16, lambda i: far_copy(peer(i), me).start())
    recv_far[me] = far[pl.ds(pl.multiple_of(24 * me, 8), 24), :]

    for load in loads[6:]:
        load.wait()

    for step, (dz, sources) in enumerate(
        ((1, (2, 3, 12, 13)), (3, (4, 5, 10, 11)), (2, (6, 7, 8, 9)), (0, (14, 15, 1)))
    ):
        for i in sources:
            vel_copy(peer(i), peer(i)).wait_recv()
        part = (z + dz) % 4

        for side in range(2):
            lanes = slice(128 * side, 128 * side + 128)
            a = 2 * part + side
            for f in range(3):
                one = recv_vel[a, :, 128 * f : 128 * f + 128]
                two = recv_vel[a + 8, :, 128 * f : 128 * f + 128]
                one_z = pltpu.roll(one, 64, 1) * dense[pl.ds(128 + a, 1), :]
                two_z = pltpu.roll(two, 64, 1) * dense[pl.ds(136 + a, 1), :]
                for r, (p, q) in enumerate(((one, two), (one_z, two_z))):
                    rows = slice(192 * r + 64 * f, 192 * r + 64 * f + 64)
                    high, low = split(p + q)
                    left_high[0, rows, lanes] = high
                    left_low[0, rows, lanes] = low
                    high, low = split(p - q)
                    left_high[1, rows, lanes] = high
                    left_low[1, rows, lanes] = low

        def inverse(n, first=step == 0, part=part):
            rows = pl.ds(pl.multiple_of(256 * part, 256), 256)
            waves = (wave[0, n, rows, :], wave[1, n, rows, :])
            term = mm3((left_high[n // 2], left_low[n // 2]), waves)
            physical[n] = term if first else physical[n] + term

        loop(0, 4, inverse)

    total[...] = jnp.zeros_like(total)
    total_far[...] = jnp.zeros_like(total_far)

    def advect(n):
        u, v, w = (physical[n, 64 * f : 64 * f + 64] for f in range(3))
        for f, field in enumerate((u, v, w)):
            slopes = mm3(gradient, split(field))
            slopes_edge[n, 24 * f : 24 * f + 24] = slopes[:24]
            slopes_edge[n, 72 + 24 * f : 96 + 24 * f] = slopes[64:88]
            spanwise = physical[n, 192 + 64 * f : 256 + 64 * f]
            product[64 * f : 64 * f + 64] = (
                keep * (u * slopes[:64] + v * slopes[64:]) + w * spanwise
            )
        total[n // 2] += mm3(split(product[...]), (back_wave[0, n], back_wave[1, n]))

    loop(0, 4, advect)

    def both(sums, rows, a):
        lanes = slice(128 * a, 128 * a + 128)
        even, odd = sums[0, rows, lanes], sums[1, rows, lanes]
        return (even + odd) * (1.0 / PLANES), (even - odd) * (1.0 / PLANES)

    def main_copy(part, p, slot):
        rows = pl.ds(*((0, FIRST), (FIRST, 192 - FIRST))[part])
        return pltpu.make_async_remote_copy(
            send_main.at[p, rows], recv_main.at[slot, rows],
            main_s.at[part, p], main_r.at[part, slot],
            device_id={"plane": p}, device_id_type=MESH,
        )

    def send_part(part):
        rows = slice(*((0, FIRST), (FIRST, 192))[part])
        for a in range(8):
            send_main[a, rows], send_main[a + 8, rows] = both(total, rows, a)
        loop(1, 16, lambda i: main_copy(part, peer(i), me).start())
        recv_main[me, rows] = send_main[me, rows]

    send_part(0)

    loop(1, 16, lambda i: far_copy(peer(i), peer(i)).wait_recv())
    for a in range(8):
        lanes = slice(128 * a, 128 * a + 128)
        for f in range(2):
            one = recv_far[a, :, 128 * f : 128 * f + 128]
            two = recv_far[a + 8, :, 128 * f : 128 * f + 128]
            rows = slice(24 * f, 24 * f + 24)
            far_modes[0, rows, lanes] = one + two
            far_modes[1, rows, lanes] = one - two

    def advect_far(n):
        velocity = mm3(split(far_modes[n // 2]), (wave[0, n], wave[1, n]))
        u, v = velocity[:24], velocity[24:]
        terms = jnp.concatenate(
            [
                u * slopes_edge[n, 24 * f : 24 * f + 24]
                + v * slopes_edge[n, 72 + 24 * f : 96 + 24 * f]
                for f in range(3)
            ],
            axis=0,
        )
        total_far[n // 2] += mm3(split(terms), (back_wave[0, n], back_wave[1, n]))

    loop(0, 4, advect_far)

    def back_copy(p, slot):
        return pltpu.make_async_remote_copy(
            send_far.at[p], shares.at[pl.ds(pl.multiple_of(24 * slot, 8), 24)],
            back_s.at[p], back_r.at[slot],
            device_id={"plane": p}, device_id_type=MESH,
        )

    for a in range(8):
        for f in range(3):
            lanes = slice(128 * f, 128 * f + 128)
            plus, minus = both(total_far, slice(24 * f, 24 * f + 24), a)
            send_far[a, :, lanes] = plus
            send_far[a + 8, :, lanes] = minus
    loop(1, 16, lambda i: back_copy(peer(i), me).start())
    shares[pl.ds(pl.multiple_of(24 * me, 8), 24), :] = send_far[me]

    loop(2, MIDDLE, lambda i: back_copy(peer(i), me).wait_send())
    send_part(1)

    loop(1, 16, lambda i: back_copy(peer(i), peer(i)).wait_recv())
    share_copies = swap(shares, 384, share_send, share_recv)
    give = jnp.where(one_hot(1152, start + turned), 0.5, 0.0).astype(jnp.bfloat16)

    for copy in share_copies:
        copy.wait_recv()
    high, low = split(shares[...])
    added[...] = mm(give, high) + mm(give, low)

    def out_copy(q):
        return pltpu.make_async_copy(out.at[q], out_hbm.at[:, :, :, pair_cols(q)], out_sem.at[q])

    def unpack(q):
        rows = pl.ds(pl.multiple_of(48 * q, 16), 48)
        for f in range(3):
            extra = added[rows, 128 * f : 128 * f + 128]
            sides = []
            for side in range(2):
                one = recv_main[2 * q + side, 64 * f : 64 * f + 64]
                sides += [one[:24] + extra[24 * side : 24 * side + 24], one[24:]]
            high, low = split(jnp.concatenate(sides, axis=0))
            block = mm(high, pair[...], TN) + mm(low, pair[...], TN)
            out[q, 0, f] = block[:64]
            out[q, 1, f] = block[64:]
        out_copy(q).start()

    def arrive(i):
        for part in range(2):
            main_copy(part, peer(i), peer(i)).wait_recv()

    def unpack_step(h):
        arrive(2 * h)
        arrive(2 * h + 1)
        unpack(peer(2 * h) // 2)

    arrive(1)
    unpack(z)
    loop(1, 8, unpack_step)

    def drain(i):
        far_copy(peer(i), me).wait_send()
        for part in range(2):
            main_copy(part, peer(i), me).wait_send()

    loop(1, 16, drain)
    vel_copy(peer(1), me).wait_send()
    back_copy(peer(1), me).wait_send()
    loop(EARLY, 16, lambda i: vel_copy(peer(i), me).wait_send())
    loop(MIDDLE, 16, lambda i: back_copy(peer(i), me).wait_send())
    for copy in trace_copies + share_copies:
        copy.wait_send()
    for q in range(8):
        out_copy(q).wait()


def shards(velocity_modes, geometry, neighbour, neighbour_edge, flipped):
    constants = [jnp.asarray(value) for value in tables()]
    anywhere = pl.BlockSpec(memory_space=pl.ANY)
    f32 = jnp.float32
    operands = (velocity_modes, geometry, neighbour.T, neighbour_edge.T, flipped.T, *constants)
    return pl.pallas_call(
        kernel,
        out_shape=jax.ShapeDtypeStruct(velocity_modes.shape, f32),
        in_specs=[anywhere] * len(operands),
        out_specs=anywhere,
        scratch_shapes=[
            pltpu.VMEM((8, 2, 3, 64, 128), f32),
        ]
        + [pltpu.VMEM(value.shape, value.dtype) for value in operands[1:]]
        + [
            pltpu.VMEM((8, 2, 3, 64, 128), f32),
            pltpu.VMEM((128, 4), f32),
            pltpu.VMEM((8, 128, 384), f32),
            pltpu.VMEM((16, 64, 384), f32),
            pltpu.VMEM((1152, 256), f32),
            pltpu.VMEM((384, 256), f32),
            pltpu.VMEM((16, 24, 256), f32),
            pltpu.VMEM((2, 384, 256), jnp.bfloat16),
            pltpu.VMEM((2, 384, 256), jnp.bfloat16),
            pltpu.VMEM((4, 384, 256), f32),
            pltpu.VMEM((384, 256), f32),
            pltpu.VMEM((2, 48, 1024), f32),
            pltpu.VMEM((4, 144, 256), f32),
            pltpu.VMEM((192, 256), f32),
            pltpu.VMEM((2, 192, 1024), f32),
            pltpu.VMEM((2, 72, 1024), f32),
            pltpu.VMEM((16, 192, 128), f32),
            pltpu.VMEM((16, 192, 128), f32),
            pltpu.VMEM((16, 24, 384), f32),
            pltpu.VMEM((1152, 384), f32),
            pltpu.VMEM((384, 384), f32),
            pltpu.SemaphoreType.REGULAR,
            pltpu.SemaphoreType.REGULAR,
            pltpu.SemaphoreType.DMA((9,)),
            pltpu.SemaphoreType.DMA((8,)),
            pltpu.SemaphoreType.DMA((8,)),
        ]
        + [pltpu.SemaphoreType.DMA((2,))] * 4
        + [pltpu.SemaphoreType.DMA((16,))] * 4
        + [pltpu.SemaphoreType.DMA((2, 16))] * 2
        + [pltpu.SemaphoreType.DMA((16,))] * 2,
        compiler_params=pltpu.CompilerParams(
            collective_id=0, has_side_effects=True, vmem_limit_bytes=56 * 2**20
        ),
    )(*operands)


def solution(mesh):
    placed = (
        P(None, None, "plane", "elem"),
        P(None, "elem"),
        P("elem", None),
        P("elem", None),
        P("elem", None),
    )
    return jax.shard_map(
        shards,
        mesh=mesh,
        in_specs=placed,
        out_specs=P(None, None, "plane", "elem"),
        check_vma=False,
    )
```

time: 108 us -> 107 us (level)
    pallas_call x1, Pallas kernels: 105 us -> 104 us  [shards(): pl.pallas_call(kernel, out_shape=jax.ShapeDtypeStruct(velocity_modes.shap...]
where the time goes in v4:
time: 107 us
  Pallas kernels  104 us (97%)
  local copies, waits for them, and re-layouts  2.73 us (3%)
    pallas_call x1, Pallas kernels, shards(): pl.pallas_call(kernel, out_shape=jax.ShapeDtypeStruct(velocity_modes.shap...  104 us
    unnamed x1, local copies, waits for them, and re-layouts  2.73 us

profile of v4, /device:TPU:8, one launch (start us, length us, event | category | flops | bytes accessed | tf_op | source)
XLA Modules:
  0.0 106.5 jit_solution(8578268275042496005)
XLA Ops:
  0.0 103.8 %shard_map.91 = f32[2,3,64,1024]{3,2,1,0:T(8,128)} custom-call(f32[2,3,64,1024]{3,2,1,0:T(8,128)} %modes_hbm.1, f32[4,1024]{1,0:T(4,128)} %geometry_hbm.1, s32[4,16]{1,0:T(4,128)} %bitcast.3, s32[4,16]{1,0:T(4,128)} %bitcast.4, s32[4,16]{1,0:T(4,128)} %bitcast.5, bf16[128,128]{1,0:T(8,128)(2,1)} %constant.8.clone.pair_hbm, ...), custom_call_target="tpu_custom_call" | custom-call | tf_op jit(solution)/shard_map/pallas_call | solution.py:517
  103.8 2.7 %copy.11 = f32[2,3,64,1024]{3,2,1,0:T(8,128)} copy(f32[2,3,64,1024]{3,2,1,0:T(8,128)} %shard_map.91) | data formatting | bytes 3145728

commit v5 on v4

--- a/solution.py
+++ b/solution.py
@@ -11,6 +11,7 @@
 POINTS = 64
 LEADER, CLERK = 2, 3
 EARLY, MIDDLE = 16, 12
+ARRIVALS = ((1, (2, 3, 12, 13)), (3, (4, 5, 10, 11)), (2, (6, 7, 8, 9)), (0, (14, 15, 1)))
 FIRST = 64
 MESH = pl.DeviceIdType.MESH
 highest = lax.Precision.HIGHEST
@@ -119,7 +120,7 @@
     out_hbm,
     modes, geometry, neighbour, neighbour_edge, flipped, pair, dense, wave, back_wave, out,
     geo_column, send_vel, recv_vel, traces, far, recv_far, left_high, left_low, physical,
-    left_far, far_modes, slopes_edge, product, total, total_far, send_main, recv_main, send_far, shares, added,
+    left_far, far_modes, far_physical, slopes_edge, product, total, total_far, send_main, recv_main, send_far, shares, added,
     plane_ok, elem_ok, load_sem, mode_sem, out_sem,
     trace_send, trace_recv, share_send, share_recv, vel_s, vel_r, far_s, far_r, main_s, main_r, back_s, back_r,
 ):
@@ -332,16 +333,17 @@
 
         lax.fori_loop(low, high, step, 0)
 
-    loop(2, EARLY, lambda i: vel_copy(peer(i), me).wait_send())
-    loop(1, 16, lambda i: far_copy(peer(i), me).start())
+    loop(2, 12, lambda i: vel_copy(peer(i), me).wait_send())
+    loop(2, 4, lambda i: far_copy(peer(i), me).start())
+    loop(12, 16, lambda i: vel_copy(peer(i), me).wait_send())
+    loop(4, 16, lambda i: far_copy(peer(i), me).start())
+    far_copy(peer(1), me).start()
     recv_far[me] = far[pl.ds(pl.multiple_of(24 * me, 8), 24), :]
 
     for load in loads[6:]:
         load.wait()
 
-    for step, (dz, sources) in enumerate(
-        ((1, (2, 3, 12, 13)), (3, (4, 5, 10, 11)), (2, (6, 7, 8, 9)), (0, (14, 15, 1)))
-    ):
+    for step, (dz, sources) in enumerate(ARRIVALS):
         for i in sources:
             vel_copy(peer(i), peer(i)).wait_recv()
         part = (z + dz) % 4
@@ -410,19 +412,30 @@
 
     send_part(0)
 
-    loop(1, 16, lambda i: far_copy(peer(i), peer(i)).wait_recv())
-    for a in range(8):
-        lanes = slice(128 * a, 128 * a + 128)
-        for f in range(2):
-            one = recv_far[a, :, 128 * f : 128 * f + 128]
-            two = recv_far[a + 8, :, 128 * f : 128 * f + 128]
-            rows = slice(24 * f, 24 * f + 24)
-            far_modes[0, rows, lanes] = one + two
-            far_modes[1, rows, lanes] = one - two
+    for step, (dz, sources) in enumerate(ARRIVALS):
+        for i in sources:
+            far_copy(peer(i), peer(i)).wait_recv()
+        part = (z + dz) % 4
+        for side in range(2):
+            lanes = slice(128 * side, 128 * side + 128)
+            a = 2 * part + side
+            for f in range(2):
+                one = recv_far[a, :, 128 * f : 128 * f + 128]
+                two = recv_far[a + 8, :, 128 * f : 128 * f + 128]
+                rows = slice(24 * f, 24 * f + 24)
+                far_modes[0, rows, lanes] = one + two
+                far_modes[1, rows, lanes] = one - two
+
+        def inverse_far(n, first=step == 0, part=part):
+            rows = pl.ds(pl.multiple_of(256 * part, 256), 256)
+            waves = (wave[0, n, rows, :], wave[1, n, rows, :])
+            term = mm3(split(far_modes[n // 2]), waves)
+            far_physical[n] = term if first else far_physical[n] + term
+
+        loop(0, 4, inverse_far)
 
     def advect_far(n):
-        velocity = mm3(split(far_modes[n // 2]), (wave[0, n], wave[1, n]))
-        u, v = velocity[:24], velocity[24:]
+        u, v = far_physical[n, :24], far_physical[n, 24:]
         terms = jnp.concatenate(
             [
                 u * slopes_edge[n, 24 * f : 24 * f + 24]
@@ -535,7 +548,8 @@
             pltpu.VMEM((2, 384, 256), jnp.bfloat16),
             pltpu.VMEM((4, 384, 256), f32),
             pltpu.VMEM((384, 256), f32),
-            pltpu.VMEM((2, 48, 1024), f32),
+            pltpu.VMEM((2, 48, 256), f32),
+            pltpu.VMEM((4, 48, 256), f32),
             pltpu.VMEM((4, 144, 256), f32),
             pltpu.VMEM((192, 256), f32),
             pltpu.VMEM((2, 192, 1024), f32),

time: 107 us -> 106 us (level)
    pallas_call x1, Pallas kernels: 104 us -> 103 us  [shards(): pl.pallas_call(kernel, out_shape=jax.ShapeDtypeStruct(velocity_modes.shap...]
where the time goes in v5:
time: 106 us; the launch traced here: 105 us
  Pallas kernels  103 us (97%)
  local copies, waits for them, and re-layouts  2.73 us (3%)
    pallas_call x1, Pallas kernels, shards(): pl.pallas_call(kernel, out_shape=jax.ShapeDtypeStruct(velocity_modes.shap...  103 us
    unnamed x1, local copies, waits for them, and re-layouts  2.73 us

profile of v5, /device:TPU:8, one launch (start us, length us, event | category | flops | bytes accessed | tf_op | source)
XLA Modules:
  0.0 105.3 jit_solution(10776257353167648889)
XLA Ops:
  0.0 102.5 %shard_map.91 = f32[2,3,64,1024]{3,2,1,0:T(8,128)} custom-call(f32[2,3,64,1024]{3,2,1,0:T(8,128)} %modes_hbm.1, f32[4,1024]{1,0:T(4,128)} %geometry_hbm.1, s32[4,16]{1,0:T(4,128)} %bitcast.3, s32[4,16]{1,0:T(4,128)} %bitcast.4, s32[4,16]{1,0:T(4,128)} %bitcast.5, bf16[128,128]{1,0:T(8,128)(2,1)} %constant.8.clone.pair_hbm, ...), custom_call_target="tpu_custom_call" | custom-call | tf_op jit(solution)/shard_map/pallas_call | solution.py:530
  102.5 2.7 %copy.11 = f32[2,3,64,1024]{3,2,1,0:T(8,128)} copy(f32[2,3,64,1024]{3,2,1,0:T(8,128)} %shard_map.91) | data formatting | bytes 3145728

commit v6 on v5

--- a/solution.py
+++ b/solution.py
@@ -9,7 +9,7 @@
 
 PLANES = 1024
 POINTS = 64
-LEADER, CLERK = 2, 3
+LEADER, CLERK = 0, 1
 EARLY, MIDDLE = 16, 12
 ARRIVALS = ((1, (2, 3, 12, 13)), (3, (4, 5, 10, 11)), (2, (6, 7, 8, 9)), (0, (14, 15, 1)))
 FIRST = 64

time: 106 us -> 106 us (level)
  no operation moved by 1% of the time
where the time goes in v6:
time: 106 us; the launch traced here: 105 us
  Pallas kernels  103 us (97%)
  local copies, waits for them, and re-layouts  2.73 us (3%)
    pallas_call x1, Pallas kernels, shards(): pl.pallas_call(kernel, out_shape=jax.ShapeDtypeStruct(velocity_modes.shap...  103 us
    unnamed x1, local copies, waits for them, and re-layouts  2.73 us

profile of v6, /device:TPU:8, one launch (start us, length us, event | category | flops | bytes accessed | tf_op | source)
XLA Modules:
  0.0 105.4 jit_solution(9218281120339655422)
XLA Ops:
  0.0 102.6 %shard_map.91 = f32[2,3,64,1024]{3,2,1,0:T(8,128)} custom-call(f32[2,3,64,1024]{3,2,1,0:T(8,128)} %modes_hbm.1, f32[4,1024]{1,0:T(4,128)} %geometry_hbm.1, s32[4,16]{1,0:T(4,128)} %bitcast.3, s32[4,16]{1,0:T(4,128)} %bitcast.4, s32[4,16]{1,0:T(4,128)} %bitcast.5, bf16[128,128]{1,0:T(8,128)(2,1)} %constant.8.clone.pair_hbm, ...), custom_call_target="tpu_custom_call" | custom-call | tf_op jit(solution)/shard_map/pallas_call | solution.py:530
  102.6 2.7 %copy.11 = f32[2,3,64,1024]{3,2,1,0:T(8,128)} copy(f32[2,3,64,1024]{3,2,1,0:T(8,128)} %shard_map.91) | data formatting | bytes 3145728
